TPU v7x, 768 devices: a whole 4x8x12 slice. The times are simulated.
768 devices in a mesh: group: 96 (over z, y), member: 8 (over x, core).
Axes of the slice: x: 4, y: 8, z: 12, core: 2. Of those that a mesh axis runs over, the one named last changes fastest.
Arguments:
- hot_table: bfloat16 [1024, 128], replicated, may hold values from -6 to 6
- warm_table: bfloat16 [8192, 128], P('member'), may hold values from -6 to 6
- cold_table: bfloat16 [98304, 128], P('group'), may hold values from -6 to 6
- warm_serve: int32 [96, 8, 8, 64], P('group', 'member'), may hold values from 0 to 1023
- cold_serve: int32 [96, 8, 96, 2], P('group', 'member'), may hold values from 0 to 1023
- feature_ids: int32 [196608, 20], P(('group', 'member')), may hold values from 0 to 1727, as said below
- labels: int32 [196608], P(('group', 'member')), may hold values 0 or 1
- cross_v: bfloat16 [2560, 256], replicated, may hold values from -0.125 to 0.125
- cross_u: bfloat16 [256, 2560], replicated, may hold values from -0.375 to 0.375
- cross_bias: float32 [2560], replicated, may hold values from -3 to 3
- w_in: bfloat16 [2560, 1024], replicated, may hold values from -0.125 to 0.125
- b_in: float32 [1024], replicated, may hold values from -3 to 3
- w_out: bfloat16 [1024], replicated, may hold values from -0.1875 to 0.1875
Outputs:
- hot_grad: float32 [1024, 128], replicated
- warm_grad: float32 [8192, 128], P('member')
- cold_grad: float32 [98304, 128], P('group')
Inputs may be any that keep to these rules, and one draw needn't show every extreme that they name: `feature_ids`: every row of each device's buffer past the hot rows is named by some lookup of that device.
All inputs are finite; a program needn't handle non-finite values. No bound on the sum of `labels` on one device may be relied on, other than what follows from the above.
Results may differ from a plain program's by a relative error of at most 0.006.
Values may be sent and summed in bfloat16 or wider, within the bound.
No kernel may reach another device: no remote copies, remote signals or barrier semaphores. Data moves between devices by JAX's collectives and lax.ppermute only.
A program may use at most 64 MiB of HBM per device.

v0:
```python
import jax
import jax.numpy as jnp
from jax import lax
from jax.sharding import PartitionSpec as P


def sample_grads(buffer, row_ids, target, cross_v, cross_u, cross_bias, w_in, b_in, w_out):
    batch_size = row_ids.shape[0]
    inputs = buffer[row_ids.reshape(-1)].reshape(batch_size, -1)
    inputs_f = inputs.astype(jnp.float32)
    narrow = jnp.dot(inputs, cross_v, preferred_element_type=jnp.float32).astype(jnp.bfloat16)
    crossed = jnp.dot(narrow, cross_u, preferred_element_type=jnp.float32) + cross_bias
    layer_one = (inputs_f * crossed + inputs_f).astype(jnp.bfloat16)
    preact = jnp.dot(layer_one, w_in, preferred_element_type=jnp.float32) + b_in
    hidden = jax.nn.silu(preact).astype(jnp.bfloat16)
    logits = jnp.dot(hidden, w_out, preferred_element_type=jnp.float32)
    d_logit = jax.nn.sigmoid(logits) - target
    gate_s = jax.nn.sigmoid(preact)
    d_hidden = (
        d_logit[:, None]
        * w_out.astype(jnp.float32)[None, :]
        * gate_s
        * (1.0 + preact * (1.0 - gate_s))
    ).astype(jnp.bfloat16)
    d_layer = jnp.dot(d_hidden, w_in.T, preferred_element_type=jnp.float32)
    d_crossed = (d_layer * inputs_f).astype(jnp.bfloat16)
    d_narrow = jnp.dot(d_crossed, cross_u.T, preferred_element_type=jnp.float32).astype(
        jnp.bfloat16
    )
    d_inputs = d_layer * (crossed + 1.0) + jnp.dot(
        d_narrow, cross_v.T, preferred_element_type=jnp.float32
    )
    return d_inputs.reshape(-1, buffer.shape[1])


def per_device(
    hot_table,
    warm_table,
    cold_table,
    warm_serve,
    cold_serve,
    feature_ids,
    labels,
    cross_v,
    cross_u,
    cross_bias,
    w_in,
    b_in,
    w_out,
):
    width = hot_table.shape[1]
    hot_rows = hot_table.shape[0]
    warm_local = warm_table.shape[0]
    cold_local = cold_table.shape[0]
    warm_list = warm_serve[0, 0]
    cold_list = cold_serve[0, 0]
    member_count = warm_list.shape[0]
    group_count = cold_list.shape[0]
    warm_slots = member_count * warm_list.shape[1]
    cold_slots = group_count * cold_list.shape[1]
    warm_wanted = warm_table[warm_list.reshape(-1)].reshape(member_count, warm_list.shape[1], width)
    warm_fetched = lax.all_to_all(warm_wanted, "member", split_axis=0, concat_axis=0, tiled=True)
    cold_wanted = cold_table[cold_list.reshape(-1)].reshape(group_count, cold_list.shape[1], width)
    cold_fetched = lax.all_to_all(cold_wanted, "group", split_axis=0, concat_axis=0, tiled=True)
    buffer = jnp.concatenate(
        [
            hot_table,
            warm_fetched.reshape(warm_slots, width),
            cold_fetched.reshape(cold_slots, width),
        ],
        axis=0,
    )
    target = labels.astype(jnp.float32)
    d_rows = sample_grads(
        buffer, feature_ids, target, cross_v, cross_u, cross_bias, w_in, b_in, w_out
    )
    summed = jax.ops.segment_sum(
        d_rows, feature_ids.reshape(-1), num_segments=hot_rows + warm_slots + cold_slots
    )
    hot_part = summed[:hot_rows]
    warm_part = summed[hot_rows : hot_rows + warm_slots].reshape(
        member_count, warm_list.shape[1], width
    )
    cold_part = summed[hot_rows + warm_slots :].reshape(group_count, cold_list.shape[1], width)
    warm_returned = lax.all_to_all(warm_part, "member", split_axis=0, concat_axis=0, tiled=True)
    warm_owned = jax.ops.segment_sum(
        warm_returned.reshape(warm_slots, width), warm_list.reshape(-1), num_segments=warm_local
    )
    cold_returned = lax.all_to_all(cold_part, "group", split_axis=0, concat_axis=0, tiled=True)
    cold_owned = jax.ops.segment_sum(
        cold_returned.reshape(cold_slots, width), cold_list.reshape(-1), num_segments=cold_local
    )
    hot_grad = lax.psum(hot_part, ("group", "member"))
    warm_grad = lax.psum(warm_owned, "group")
    cold_grad = lax.psum(cold_owned, "member")
    return (hot_grad, warm_grad, cold_grad)


def solution(mesh):
    placed = (
        P(),
        P("member", None),
        P("group", None),
        P("group", "member", None, None),
        P("group", "member", None, None),
        P(("group", "member"), None),
        P(("group", "member")),
        P(),
        P(),
        P(),
        P(),
        P(),
        P(),
    )
    return jax.shard_map(
        per_device,
        mesh=mesh,
        in_specs=placed,
        out_specs=(P(), P("member", None), P("group", None)),
        check_vma=False,
    )
```

profile of v0, /device:TPU:1, one launch (start us, length us, event | category | flops | bytes accessed | tf_op | source)
XLA Modules:
  0.0 925.2 jit_solution(10840555764020459567)
XLA Ops:
  7.2 0.0 copy-start
  7.2 0.0 copy-start.1
  7.2 0.9 reshape_squeeze.6
  8.1 2.6 gather_fusion
  10.7 13.8 %all-to-all-start = ((bf16[8,64,128]{2,1,0:T(8,128)(2,1)}), bf16[8,64,128]{2,1,0:T(8,128)(2,1)S(1)}, u32[]{:S(2)}, u32[]{:S(2)}) async-start(bf16[8,64,128]{2,1,0:T(8,128)(2,1)} %bitcast.1), calls=%async_computation | async-start | bytes 262144 | tf_op jit(solution)/shard_map/all_to_all | solution.py:62
  24.5 0.8 copy.17
  25.3 0.1 reshape_squeeze.7
  25.4 0.8 copy.16
  26.3 0.1 broadcast_in_dim_reshape.3
  26.5 0.7 convert_element_type.32
  27.2 0.7 reshape.186
  27.8 0.1 reshape.161
  28.0 2.3 gather_fusion.1
  30.3 0.0 all-to-all-done
  30.3 13.7 %all-to-all-start.1 = ((bf16[96,2,128]{2,1,0:T(2,128)(2,1)}), bf16[96,2,128]{2,1,0:T(2,128)(2,1)S(1)}, u32[]{:S(2)}, u32[]{:S(2)}) async-start(bf16[96,2,128]{2,1,0:T(2,128)(2,1)} %bitcast.4), calls=%async_computation.1 | async-start | bytes 98304 | tf_op jit(solution)/shard_map/all_to_all | solution.py:64
  44.0 12.9 %all-to-all-done.1 = bf16[96,2,128]{2,1,0:T(2,128)(2,1)S(1)} async-done(((bf16[96,2,128]{2,1,0:T(2,128)(2,1)}), bf16[96,2,128]{2,1,0:T(2,128)(2,1)S(1)}, u32[]{:S(2)}, u32[]{:S(2)}) %all-to-all-start.1) | async-done | bytes 49184 | tf_op jit(solution)/shard_map/all_to_all | solution.py:64
  56.9 0.0 copy-done.1
  57.0 18.6 %gather_fusion.2 = bf16[5120,128]{1,0:T(8,128)(2,1)} fusion(bf16[1728,128]{1,0:T(8,128)(2,1)S(1)} %pad_maximum_fusion, s32[5120]{0:T(1024)S(1)} %broadcast_clamp_fusion), kind=kCustom, calls=%fused_computation.2 | custom fusion | bytes 2641920 | tf_op jit(solution)/shard_map/gather | solution.py:9
  75.6 0.0 copy-start.3
  75.6 2.9 reshape.129
  78.5 0.0 copy-done
  78.5 0.0 copy-done.3
  78.5 0.0 copy-start.5
  78.5 4.4 convolution_add_fusion.1
  82.9 0.0 copy-done.5
  82.9 4.8 fusion.6
  87.7 0.0 copy-start.4
  87.7 0.4 fusion.18
  88.1 0.3 copy-done.4
  88.4 5.9 fusion.14
  94.3 6.8 convolution_add_fusion
  101.1 3.6 reshape.163
  104.7 0.0 copy-start.2
  104.7 28.5 %scatter_custom_fusion = f32[1728,128]{1,0:T(8,128)S(1)} fusion(s32[5120]{0:T(1024)S(1)} %reshape.161, f32[5120,128]{1,0:T(8,128)} %reshape.163, f32[]{:T(128)} %constant.5.clone.1), kind=kCustom, calls=%fused_computation.26 | custom fusion | flops 655360 | bytes 885248 | tf_op jit(solution)/shard_map/scatter-add | solution.py:77
  133.1 0.6 slice.20
  133.8 5.9 all-to-all-start.3
  139.7 0.0 all-reduce.4.cloned.1.call-start
  139.8 0.8 slice.18
  140.6 0.0 all-reduce.4.cloned.1.call-update
  140.6 0.0 all-reduce.8.cloned.1.call-start
  140.7 0.1 reshape.177
  140.8 12.4 %all-to-all-done.3 = f32[96,2,128]{2,1,0:T(2,128)S(1)} async-done(((f32[96,2,128]{2,1,0:T(2,128)}), f32[96,2,128]{2,1,0:T(2,128)S(1)}, u32[]{:S(2)}, u32[]{:S(2)}) %all-to-all-start.3) | async-done | bytes 98336 | tf_op jit(solution)/shard_map/all_to_all | solution.py:89
  153.2 2.0 scatter_custom_fusion.2
  155.2 0.0 all-reduce.8.cloned.1.call-update
  155.3 0.7 slice.19
  156.0 7.4 all-to-all-start.2
  163.4 0.0 all-reduce.6.cloned.1.call-start
  163.4 0.0 copy-done.2
  163.4 0.1 reshape.169
  163.5 6.5 all-to-all-done.2
  170.0 3.0 scatter_custom_fusion.1
  173.0 0.0 all-reduce.6.cloned.1.call-update
  173.0 436.6 %all-reduce.4.cloned.1.call-done = f32[1024,128]{1,0:T(8,128)} async-done(((f32[1024,128]{1,0:T(8,128)}), f32[1024,128]{1,0:T(8,128)}) %all-reduce.4.cloned.1.call-update) | async-done | bytes 524304 | tf_op jit(solution)/shard_map/psum | solution.py:93
  609.6 77.2 %all-reduce.8.cloned.1.call-done = f32[1024,128]{1,0:T(8,128)} async-done(((f32[1024,128]{1,0:T(8,128)}), f32[1024,128]{1,0:T(8,128)}) %all-reduce.8.cloned.1.call-update) | async-done | bytes 524304 | tf_op jit(solution)/shard_map/psum | solution.py:95
  686.8 226.2 %all-reduce.6.cloned.1.call-done = f32[1024,128]{1,0:T(8,128)} async-done(((f32[1024,128]{1,0:T(8,128)}), f32[1024,128]{1,0:T(8,128)}) %all-reduce.6.cloned.1.call-update) | async-done | bytes 524304 | tf_op jit(solution)/shard_map/psum | solution.py:94
  913.0 1.9 copy.23
  914.9 1.9 copy.24
  916.8 1.9 copy.25
  (8 shorter events, 0.1 us)
Async XLA Ops:
  7.2 71.3 %copy-start = (bf16[2560,256]{1,0:T(8,128)(2,1)S(1)}, bf16[2560,256]{1,0:T(8,128)(2,1)}, u32[]{:S(2)}) copy-start(bf16[2560,256]{1,0:T(8,128)(2,1)} %param.20) | copy-start | bytes 3932164
  7.2 49.7 %copy-start.1 = (bf16[1024,128]{1,0:T(8,128)(2,1)S(1)}, bf16[1024,128]{1,0:T(8,128)(2,1)}, u32[]{:S(2)}) copy-start(bf16[1024,128]{1,0:T(8,128)(2,1)} %param.13) | copy-start | bytes 786436
  10.7 19.5 %all-to-all-start = ((bf16[8,64,128]{2,1,0:T(8,128)(2,1)}), bf16[8,64,128]{2,1,0:T(8,128)(2,1)S(1)}, u32[]{:S(2)}, u32[]{:S(2)}) async-start(bf16[8,64,128]{2,1,0:T(8,128)(2,1)} %bitcast.1), calls=%async_computation | async-start | bytes 262144 | tf_op jit(solution)/shard_map/all_to_all | solution.py:62
  30.3 26.7 %all-to-all-start.1 = ((bf16[96,2,128]{2,1,0:T(2,128)(2,1)}), bf16[96,2,128]{2,1,0:T(2,128)(2,1)S(1)}, u32[]{:S(2)}, u32[]{:S(2)}) async-start(bf16[96,2,128]{2,1,0:T(2,128)(2,1)} %bitcast.4), calls=%async_computation.1 | async-start | bytes 98304 | tf_op jit(solution)/shard_map/all_to_all | solution.py:64
  75.6 2.9 copy-start.3
  78.5 4.4 copy-start.5
  87.7 0.7 copy-start.4
  104.7 58.7 %copy-start.2 = (s32[1,1,8,64]{3,2,1,0:T(8,128)S(1)}, s32[1,1,8,64]{3,2,1,0:T(8,128)}, u32[]{:S(2)}) copy-start(s32[1,1,8,64]{3,2,1,0:T(8,128)} %param.16) | copy-start | bytes 6148
  133.8 19.5 %all-to-all-start.3 = ((f32[96,2,128]{2,1,0:T(2,128)}), f32[96,2,128]{2,1,0:T(2,128)S(1)}, u32[]{:S(2)}, u32[]{:S(2)}) async-start(f32[96,2,128]{2,1,0:T(2,128)} %bitcast.10), calls=%async_computation.3 | async-start | bytes 196608 | tf_op jit(solution)/shard_map/all_to_all | solution.py:89
  139.7 469.9 %all-reduce.4.cloned.1.call-start = ((), (), s32[]{:S(2)}) async-start(), calls=%async_computation.4 | async-start | bytes 1048576 | tf_op jit(solution)/shard_map/psum | solution.py:93
  140.6 546.2 %all-reduce.8.cloned.1.call-start = ((), (), s32[]{:S(2)}) async-start(), calls=%async_computation.6 | async-start | bytes 1048576 | tf_op jit(solution)/shard_map/psum | solution.py:95
  156.0 14.0 %all-to-all-start.2 = ((f32[8,64,128]{2,1,0:T(8,128)}), f32[8,64,128]{2,1,0:T(8,128)S(1)}, u32[]{:S(2)}, u32[]{:S(2)}) async-start(f32[8,64,128]{2,1,0:T(8,128)} %bitcast.8), calls=%async_computation.2 | async-start | bytes 524288 | tf_op jit(solution)/shard_map/all_to_all | solution.py:85
  163.4 749.7 %all-reduce.6.cloned.1.call-start = ((), (), s32[]{:S(2)}) async-start(), calls=%async_computation.5 | async-start | bytes 1048576 | tf_op jit(solution)/shard_map/psum | solution.py:94
Sparse Core Ops, SparseCore 0:
  146.5 463.0 all-reduce.3
  612.6 74.1 all-reduce.7
  691.0 221.9 all-reduce.5
where the time goes:
time: 932 us; the launch traced here: 925 us
  waiting for transfers between devices  772 us (83%)
  local copies, waits for them, and re-layouts  41.9 us (4%)
  starting transfers between devices  40.9 us (4%)
  other arithmetic  34.3 us (4%)
  matrix products  22.2 us (2%)
  between operations  13.9 us (1%)
    psum x1, waiting for transfers between devices, per_device(): hot_grad = lax.psum(hot_part, ('group', 'member'))  437 us
    psum x1, waiting for transfers between devices, per_device(): warm_grad = lax.psum(warm_owned, 'group')  226 us
    psum x1, waiting for transfers between devices, per_device(): cold_grad = lax.psum(cold_owned, 'member')  77.2 us
    scatter-add x1, other arithmetic, per_device(): jax.ops.segment_sum(d_rows, feature_ids.reshape(-1), num_segments=hot_row...  28.5 us
  transfers between devices with their start and end apart: 7, of which 6 were waited for; matrix products, arithmetic and copies ran while one was open for 1% of the time, Pallas kernels for 0%

commit v1 on v0

v1 whole, which is shorter than its diff:
```python
import functools

import jax
import jax.numpy as jnp
from jax import lax
from jax.experimental import pallas as pl
from jax.experimental.pallas import tpu as pltpu
from jax.sharding import PartitionSpec as P

F32 = jnp.float32
BF16 = jnp.bfloat16
VMEM = pl.BlockSpec(memory_space=pltpu.VMEM)
ANY = pl.BlockSpec(memory_space=pl.ANY)
TILE = 256


def up(value, step):
    return (value + step - 1) // step * step


def iota(shape, axis):
    return lax.broadcasted_iota(jnp.int32, shape, axis)


def hits(left, right):
    return jnp.where(left == right, 1.0, 0.0).astype(BF16)


def dot(a, b):
    return jnp.dot(a, b, preferred_element_type=F32)


def dot_nt(a, b):
    return lax.dot_general(a, b, (((1,), (1,)), ((), ())), preferred_element_type=F32)


def column_of(row):
    size = row.shape[1]
    same = iota((size, size), 0) == iota((size, size), 1)
    return jnp.sum(jnp.where(same, row, 0), axis=1, keepdims=True)


def row_of(column):
    size = column.shape[0]
    same = iota((size, size), 0) == iota((size, size), 1)
    return jnp.sum(jnp.where(same, column, 0), axis=0, keepdims=True)


def tower_kernel(
    hot_ref, warm_ref, cold_ref, ids_ref, label_ref, bias_ref, b_in_ref, w_out_ref,
    v_hbm, u_hbm, w_hbm,
    member_ref, cold_out_ref,
    table, turned, inputs, crossed, d_layer, narrow, preact, total, v_ref, u_ref, w_ref, sems,
):
    copies = [
        pltpu.make_async_copy(v_hbm, v_ref, sems.at[0]),
        pltpu.make_async_copy(u_hbm, u_ref, sems.at[1]),
        pltpu.make_async_copy(w_hbm, w_ref, sems.at[2]),
    ]
    for copy in copies:
        copy.start()
    batch = ids_ref.shape[0]
    width = hot_ref.shape[1]
    fields = ids_ref.shape[1]
    steps = inputs.shape[1] // TILE
    each = TILE // width
    hot_rows = hot_ref.shape[0]
    warm_rows = warm_ref.shape[0]
    cold_rows = cold_ref.shape[0]
    slots = hot_rows + warm_rows + cold_rows
    table[0:hot_rows, :] = hot_ref[...]
    table[hot_rows : hot_rows + warm_rows, :] = warm_ref[...]
    table[hot_rows + warm_rows : slots, :] = cold_ref[...]

    def cols(step):
        return pl.ds(pl.multiple_of(step * TILE, TILE), TILE)

    narrow[...] = jnp.zeros_like(narrow)
    copies[0].wait()

    @pl.loop(0, steps)
    def _(step):
        pieces = []
        for k in range(each):
            field = step * each + k
            ids = jnp.sum(
                jnp.where(iota((batch, fields), 1) == field, ids_ref[...], 0), axis=1, keepdims=True
            )
            turned[pl.ds(field, 1), :] = row_of(ids)
            chosen = hits(iota((batch, slots), 1), ids)
            pieces.append(dot(chosen, table[...]).astype(BF16))
        part = jnp.concatenate(pieces, axis=1)
        inputs[:, cols(step)] = part
        narrow[...] += dot(part, v_ref[cols(step), :])

    low = narrow[...].astype(BF16)
    preact[...] = jnp.zeros_like(preact)
    copies[1].wait()
    copies[2].wait()

    @pl.loop(0, steps)
    def _(step):
        part = inputs[:, cols(step)].astype(F32)
        cross = dot(low, u_ref[:, cols(step)]) + bias_ref[:, cols(step)]
        crossed[:, cols(step)] = cross
        layer_one = (part * cross + part).astype(BF16)
        preact[...] += dot(layer_one, w_ref[cols(step), :])

    pre = preact[...] + b_in_ref[...]
    gate = jax.nn.sigmoid(pre)
    w_out = w_out_ref[...].astype(F32)
    hidden = (pre * gate).astype(BF16).astype(F32)
    logits = jnp.sum(hidden * w_out, axis=1, keepdims=True)
    d_logit = jax.nn.sigmoid(logits) - column_of(label_ref[...].astype(F32))
    d_hidden = (d_logit * w_out * gate * (1.0 + pre * (1.0 - gate))).astype(BF16)
    narrow[...] = jnp.zeros_like(narrow)

    @pl.loop(0, steps)
    def _(step):
        part = inputs[:, cols(step)].astype(F32)
        d_part = dot_nt(d_hidden, w_ref[cols(step), :])
        d_layer[:, cols(step)] = d_part
        d_crossed = (d_part * part).astype(BF16)
        narrow[...] += dot_nt(d_crossed, u_ref[:, cols(step)])

    d_low = narrow[...].astype(BF16)
    total[...] = jnp.zeros_like(total)

    @pl.loop(0, steps)
    def _(step):
        d_in = d_layer[:, cols(step)] * (crossed[:, cols(step)] + 1.0)
        d_in += dot_nt(d_low, v_ref[cols(step), :])
        high = d_in.astype(BF16)
        rest = (d_in - high.astype(F32)).astype(BF16)
        places, values = [], []
        for k in range(each):
            ids = turned[pl.ds(step * each + k, 1), :]
            places.append(hits(iota((slots, batch), 0), ids))
            piece = slice(k * width, (k + 1) * width)
            values.append(jnp.concatenate([high[:, piece], rest[:, piece]], axis=1))
        total[...] += dot(jnp.concatenate(places, axis=1), jnp.concatenate(values, axis=0))

    members = member_ref.shape[0]
    hot_each = hot_rows // members
    warm_each = warm_rows // members

    def rows(start, size):
        return (total[start : start + size, :width] + total[start : start + size, width:]).astype(BF16)

    for m in range(members):
        member_ref[m, 0:hot_each, :] = rows(m * hot_each, hot_each)
        member_ref[m, hot_each : hot_each + warm_each, :] = rows(hot_rows + m * warm_each, warm_each)
    cold_out_ref[...] = rows(hot_rows + warm_rows, cold_rows)


def tower(hot, warm, cold, ids, labels, bias, b_in, w_out, v, u, w, members):
    batch, fields = ids.shape
    width = hot.shape[1]
    wide, rank = v.shape
    hid = w.shape[1]
    slots = hot.shape[0] + warm.shape[0] + cold.shape[0]
    each = (hot.shape[0] + warm.shape[0]) // members
    flops = 2 * batch * wide * (2 * rank + hid) * 2 + 4 * batch * fields * slots * width * 2
    return pl.pallas_call(
        tower_kernel,
        name="tower",
        out_shape=(
            jax.ShapeDtypeStruct((members, each, width), BF16),
            jax.ShapeDtypeStruct(cold.shape, BF16),
        ),
        in_specs=[VMEM] * 8 + [ANY] * 3,
        out_specs=(VMEM, VMEM),
        scratch_shapes=[
            pltpu.VMEM((slots, width), BF16),
            pltpu.VMEM((up(fields, 8), batch), jnp.int32),
            pltpu.VMEM((batch, wide), BF16),
            pltpu.VMEM((batch, wide), F32),
            pltpu.VMEM((batch, wide), F32),
            pltpu.VMEM((batch, rank), F32),
            pltpu.VMEM((batch, hid), F32),
            pltpu.VMEM((slots, 2 * width), F32),
            pltpu.VMEM(v.shape, BF16),
            pltpu.VMEM(u.shape, BF16),
            pltpu.VMEM(w.shape, BF16),
            pltpu.SemaphoreType.DMA((3,)),
        ],
        compiler_params=pltpu.CompilerParams(vmem_limit_bytes=40 * 2**20),
        cost_estimate=pl.CostEstimate(flops=flops, bytes_accessed=10_000_000, transcendentals=batch * hid),
    )(hot, warm, cold, ids, labels, bias, b_in, w_out, v, u, w)


def call(kernel, name, out_shape, args, flops):
    single = isinstance(out_shape, jax.ShapeDtypeStruct)
    return pl.pallas_call(
        kernel,
        name=name,
        out_shape=out_shape,
        in_specs=[VMEM] * len(args),
        out_specs=VMEM if single else tuple(VMEM for _ in out_shape),
        compiler_params=pltpu.CompilerParams(vmem_limit_bytes=32 * 2**20),
        cost_estimate=pl.CostEstimate(flops=flops, bytes_accessed=2_000_000, transcendentals=0),
    )(*args)


def owner_kernel(chunk, slot, groups, keep, got_ref, cold_ref, to_ref, out_ref):
    out_rows = groups * slot
    place = iota((out_rows, 1), 0)
    group, at = place // slot, place % slot
    keeps = keep // groups
    wanted = jnp.where(at < chunk, group * chunk + at, -1)
    cold_wanted = jnp.where((at >= chunk) & (at < chunk + keeps), group * keeps + at - chunk, -1)
    out = dot(hits(wanted, to_ref[...]), got_ref[...])
    out += dot(hits(cold_wanted, iota((out_rows, keep), 1)), cold_ref[...])
    out_ref[...] = out.astype(BF16)


def finish_kernel(chunk, keeps, got_ref, chunk_ref, cold_ref):
    groups, slot, width = got_ref.shape
    summed = jnp.sum(got_ref[...].astype(F32), axis=0)
    chunk_ref[...] = jnp.broadcast_to(summed.astype(BF16)[None], chunk_ref.shape)
    cold_rows = cold_ref.shape[0]
    place = iota((cold_rows, 1), 0)
    wanted = place // keeps * slot + chunk + place % keeps
    flat = got_ref[...].reshape(groups * slot, width)
    cold_ref[...] = dot(hits(wanted, iota((cold_rows, groups * slot), 1)), flat).astype(BF16)


def spread_kernel(chunk, got_ref, cold_ref, warm_ref, out_ref):
    groups, slot, width = got_ref.shape
    members = out_ref.shape[0]
    warm_rows = warm_ref.shape[0]
    cold_rows = cold_ref.shape[0]
    hot_each = out_ref.shape[1] - cold_rows
    flat = got_ref[...].reshape(groups * slot, width)

    def pick(start, rows):
        place = iota((rows, 1), 0) + start
        wanted = place // chunk * slot + place % chunk
        return dot(hits(wanted, iota((rows, groups * slot), 1)), flat)

    warm_ref[...] = pick(0, warm_rows)
    hot = pick(warm_rows, hot_each).astype(BF16)
    for m in range(members):
        out_ref[m, 0:hot_each, :] = hot
        out_ref[m, hot_each : hot_each + cold_rows, :] = cold_ref[...]


def last_kernel(got_ref, to_ref, hot_ref, cold_ref):
    members, each, width = got_ref.shape
    hot_each = hot_ref.shape[0] // members
    cold_local = cold_ref.shape[0]
    rows = []
    for m in range(members):
        hot_ref[m * hot_each : (m + 1) * hot_each, :] = got_ref[m, 0:hot_each, :].astype(F32)
        rows.append(got_ref[m, hot_each:each, :])
    flat = jnp.concatenate(rows, axis=0)
    cold_ref[...] = dot(hits(iota((cold_local, flat.shape[0]), 0), to_ref[...]), flat)


def per_device(
    hot_table, warm_table, cold_table, warm_serve, cold_serve, feature_ids, labels,
    cross_v, cross_u, cross_bias, w_in, b_in, w_out,
):
    width = hot_table.shape[1]
    hot_rows = hot_table.shape[0]
    warm_local = warm_table.shape[0]
    cold_local = cold_table.shape[0]
    warm_list = warm_serve[0, 0]
    cold_list = cold_serve[0, 0]
    members, wcap = warm_list.shape
    groups, ccap = cold_list.shape
    warm_slots = members * wcap
    cold_slots = groups * ccap
    hot_each = hot_rows // members
    chunk = up(warm_local + hot_each, groups) // groups
    slot = up(chunk + ccap, 16)

    def exchange(x, axis):
        return lax.all_to_all(x, axis, split_axis=0, concat_axis=0, tiled=True)

    cold_to = lax.all_gather(cold_list.reshape(1, cold_slots), "member", axis=1, tiled=True)
    warm_wanted = warm_table[warm_list.reshape(-1)].reshape(members, wcap, width)
    warm_fetched = exchange(warm_wanted, "member").reshape(warm_slots, width)
    cold_wanted = cold_table[cold_list.reshape(-1)].reshape(groups, ccap, width)
    cold_fetched = exchange(cold_wanted, "group").reshape(cold_slots, width)

    to_members, cold_part = tower(
        hot_table, warm_fetched, cold_fetched, feature_ids, labels.reshape(1, -1),
        cross_bias.reshape(1, -1), b_in.reshape(1, -1), w_out.reshape(1, -1),
        cross_v, cross_u, w_in, members,
    )
    got = exchange(to_members, "member")

    hot_to = jnp.broadcast_to(warm_local + jnp.arange(hot_each, dtype=jnp.int32)[None], (members, hot_each))
    row_to = jnp.concatenate([hot_to, warm_list], axis=1).reshape(1, -1)
    to_groups = call(
        functools.partial(owner_kernel, chunk, slot, groups, cold_slots),
        "owner",
        jax.ShapeDtypeStruct((groups * slot, width), BF16),
        (got.reshape(-1, width), cold_part, row_to),
        2 * groups * slot * width * (row_to.shape[1] + cold_slots),
    )
    summands = exchange(to_groups.reshape(groups, slot, width), "group")
    my_chunk, my_cold = call(
        functools.partial(finish_kernel, chunk, ccap),
        "finish",
        (
            jax.ShapeDtypeStruct((groups, slot, width), BF16),
            jax.ShapeDtypeStruct((cold_slots, width), BF16),
        ),
        (summands,),
        2 * groups * slot * width * cold_slots,
    )
    chunks = exchange(my_chunk, "group")
    warm_grad, to_all = call(
        functools.partial(spread_kernel, chunk),
        "spread",
        (
            jax.ShapeDtypeStruct((warm_local, width), F32),
            jax.ShapeDtypeStruct((members, hot_each + cold_slots, width), BF16),
        ),
        (chunks, my_cold),
        2 * groups * slot * width * (warm_local + hot_each),
    )
    last = exchange(to_all, "member")
    hot_grad, cold_grad = call(
        last_kernel,
        "last",
        (
            jax.ShapeDtypeStruct((hot_rows, width), F32),
            jax.ShapeDtypeStruct((cold_local, width), F32),
        ),
        (last, cold_to),
        2 * cold_local * members * cold_slots * width,
    )
    return hot_grad, warm_grad, cold_grad


def solution(mesh):
    placed = (
        P(),
        P("member", None),
        P("group", None),
        P("group", "member", None, None),
        P("group", "member", None, None),
        P(("group", "member"), None),
        P(("group", "member")),
        P(),
        P(),
        P(),
        P(),
        P(),
        P(),
    )
    return jax.shard_map(
        per_device,
        mesh=mesh,
        in_specs=placed,
        out_specs=(P(), P("member", None), P("group", None)),
        check_vma=False,
    )
```

time: 932 us -> 178 us (0.19)
  waiting for transfers between devices: 772 us -> 24.3 us
  blocking collectives: 0 us -> 64.5 us
  Pallas kernels: 0 us -> 36 us
  other arithmetic: 34.3 us -> 0.04 us
  local copies, waits for them, and re-layouts: 41.9 us -> 10.2 us
  matrix products: 22.2 us -> 0 us
  between operations: 13.9 us -> 1.54 us
    psum x3 -> x0, waiting for transfers between devices: 740 us -> none  [the longest x1 437 us: per_device(): hot_grad = lax.psum(hot_part, ('group', 'member'))]
    all_to_all x0 -> x2, blocking collectives: none -> 54.1 us  [exchange(): return lax.all_to_all(x, axis, split_axis=0, concat_axis=0, tiled=True)]
    pallas_call x0 -> x5, Pallas kernels: none -> 36 us  [the longest x1 29.9 us: tower(): pl.pallas_call(tower_kernel, name='tower', out_shape=(jax.ShapeDtypeStruc...]
    scatter-add x3 -> x0, other arithmetic: 33.5 us -> none  [the longest x1 28.5 us: per_device(): jax.ops.segment_sum(d_rows, feature_ids.reshape(-1), num_segments=hot_row...]
    dot_general x5 -> x0, matrix products: 22.2 us -> none  [the longest x1 6.78 us: sample_grads(): jnp.dot(d_narrow, cross_v.T, preferred_element_type=jnp.float32)]
    gather x3 -> x2, local copies, waits for them, and re-layouts: 23.6 us -> 3.31 us  [the longest x1 1.92 us: per_device(): warm_table[warm_list.reshape(-1)].reshape(members, wcap, width)]
    unnamed x0 -> x1, blocking collectives: none -> 10.4 us
  transfers between devices with their start and end apart: 7 -> 4, of which waited for: 6 -> 3; matrix products, arithmetic and copies ran while one was open for 1% -> 2% of each run, Pallas kernels for 0% -> 0%
where the time goes in v1:
time: 178 us
  blocking collectives  64.5 us (36%)
  starting transfers between devices  41 us (23%)
  Pallas kernels  36 us (20%)
  waiting for transfers between devices  24.3 us (14%)
  local copies, waits for them, and re-layouts  10.2 us (6%)
    all_to_all x2, blocking collectives, exchange(): return lax.all_to_all(x, axis, split_axis=0, concat_axis=0, tiled=True)  54.1 us
    all_to_all x4, starting transfers between devices, exchange(): return lax.all_to_all(x, axis, split_axis=0, concat_axis=0, tiled=True)  41 us
    pallas_call x1, Pallas kernels, tower(): pl.pallas_call(tower_kernel, name='tower', out_shape=(jax.ShapeDtypeStruc...  29.9 us
    all_to_all x4, waiting for transfers between devices, exchange(): return lax.all_to_all(x, axis, split_axis=0, concat_axis=0, tiled=True)  24.3 us
    unnamed x1, blocking collectives  10.4 us
    pallas_call x4, Pallas kernels, call(): pl.pallas_call(kernel, name=name, out_shape=out_shape, in_specs=[VMEM] *...  6.06 us
    unnamed x33, local copies, waits for them, and re-layouts  5.77 us
  transfers between devices with their start and end apart: 4, of which 3 were waited for; matrix products, arithmetic and copies ran while one was open for 2% of the time, Pallas kernels for 0%

profile of v1, /device:TPU:1, one launch (start us, length us, event | category | flops | bytes accessed | tf_op | source)
XLA Modules:
  0.0 177.6 jit_solution(3188800761244505267)
XLA Ops:
  0.6 0.0 copy-start
  0.6 0.0 copy-start.12
  0.7 0.0 copy-start.7
  0.7 0.0 copy-start.11
  0.7 0.0 copy-start.10
  0.7 0.0 copy-start.8
  0.7 0.0 copy-start.5
  0.7 0.0 copy-start.2
  0.7 0.0 copy-start.6
  0.7 0.0 copy-start.4
  0.7 0.9 reshape_squeeze.9
  1.7 0.0 copy-done
  1.7 1.9 %gather_fusion = bf16[512,128]{1,0:T(8,128)(2,1)} fusion(bf16[1024,128]{1,0:T(8,128)(2,1)S(1)} %copy-done, s32[1024]{0:T(1024)S(1)} %pad_clamp_fusion.1), kind=kCustom, calls=%fused_computation | custom fusion | bytes 264192 | tf_op jit(solution)/shard_map/gather | solution.py:282
  3.6 13.8 %all-to-all-start = ((bf16[8,64,128]{2,1,0:T(8,128)(2,1)}), bf16[8,64,128]{2,1,0:T(8,128)(2,1)S(1)}, u32[]{:S(2)}, u32[]{:S(2)}) async-start(bf16[8,64,128]{2,1,0:T(8,128)(2,1)} %bitcast.1), calls=%async_computation | async-start | bytes 262144 | tf_op jit(solution)/shard_map/all_to_all | solution.py:279
  17.4 0.0 copy-done.12
  17.4 0.1 copy.17
  17.5 0.1 reshape_squeeze.10
  17.6 0.0 copy-done.7
  17.6 1.4 gather_fusion.1
  19.0 3.6 %all-to-all-done = bf16[8,64,128]{2,1,0:T(8,128)(2,1)S(1)} async-done(((bf16[8,64,128]{2,1,0:T(8,128)(2,1)}), bf16[8,64,128]{2,1,0:T(8,128)(2,1)S(1)}, u32[]{:S(2)}, u32[]{:S(2)}) %all-to-all-start) | async-done | bytes 131104 | tf_op jit(solution)/shard_map/all_to_all | solution.py:279
  22.7 13.7 %all-to-all-start.1 = ((bf16[96,2,128]{2,1,0:T(2,128)(2,1)}), bf16[96,2,128]{2,1,0:T(2,128)(2,1)S(1)}, u32[]{:S(2)}, u32[]{:S(2)}) async-start(bf16[96,2,128]{2,1,0:T(2,128)(2,1)} %bitcast.4), calls=%async_computation.1 | async-start | bytes 98304 | tf_op jit(solution)/shard_map/all_to_all | solution.py:279
  36.4 0.0 copy-done.11
  36.4 0.0 copy-done.10
  36.4 0.0 copy-done.8
  36.4 0.1 copy.18.ids_ref
  36.6 12.7 %all-to-all-done.1 = bf16[96,2,128]{2,1,0:T(2,128)(2,1)S(1)} async-done(((bf16[96,2,128]{2,1,0:T(2,128)(2,1)}), bf16[96,2,128]{2,1,0:T(2,128)(2,1)S(1)}, u32[]{:S(2)}, u32[]{:S(2)}) %all-to-all-start.1) | async-done | bytes 49184 | tf_op jit(solution)/shard_map/all_to_all | solution.py:279
  49.3 0.0 copy-done.5
  49.3 0.0 copy-done.2
  49.3 0.0 copy-done.6
  49.3 0.0 copy-done.4
  49.3 0.0 copy-start.1
  49.3 2.5 %copy-done.1 = bf16[2560,1024]{1,0:T(8,128)(2,1)S(1)} copy-done((bf16[2560,1024]{1,0:T(8,128)(2,1)S(1)}, bf16[2560,1024]{1,0:T(8,128)(2,1)}, u32[]{:S(2)}) %copy-start.1) | copy-done | bytes 5242904
  51.8 0.0 copy-start.3
  51.8 1.3 copy-done.3
  53.1 0.0 copy-start.9
  53.1 29.9 %tower.1 = (bf16[8,192,128]{2,1,0:T(8,128)(2,1)}, bf16[192,128]{1,0:T(8,128)(2,1)S(1)}) custom-call(bf16[1024,128]{1,0:T(8,128)(2,1)S(1)} %copy-done.4, bf16[512,128]{1,0:T(8,128)(2,1)S(1)} %bitcast.20, bf16[192,128]{1,0:T(8,128)(2,1)S(1)} %bitcast.21, s32[256,20]{1,0:T(8,128)S(1)} %copy.18.ids_ref, s32[1,256]{1,0:T(1,128)S(1)} %bitcast.23, ...), custom_call_target="tpu_custom_call" | custom-call | flops 13086228480 | bytes 10000000 | tf_op jit(solution)/shard_map/tower/pallas_call | solution.py:164
  83.1 5.7 %all-to-all-start.2 = ((bf16[8,192,128]{2,1,0:T(8,128)(2,1)}), bf16[8,192,128]{2,1,0:T(8,128)(2,1)S(1)}, u32[]{:S(2)}, u32[]{:S(2)}) async-start(bf16[8,192,128]{2,1,0:T(8,128)(2,1)} %get-tuple-element.11), calls=%async_computation.2 | async-start | bytes 786432 | tf_op jit(solution)/shard_map/all_to_all | solution.py:279
  88.8 0.0 copy-done.9
  88.8 0.1 reshape.109.to_ref
  88.9 8.0 %all-to-all-done.2 = bf16[8,192,128]{2,1,0:T(8,128)(2,1)S(1)} async-done(((bf16[8,192,128]{2,1,0:T(8,128)(2,1)}), bf16[8,192,128]{2,1,0:T(8,128)(2,1)S(1)}, u32[]{:S(2)}, u32[]{:S(2)}) %all-to-all-start.2) | async-done | bytes 393248 | tf_op jit(solution)/shard_map/all_to_all | solution.py:279
  96.9 1.6 owner.1
  98.5 26.8 %all_to_all.30.got_ref = bf16[96,16,128]{2,1,0:T(8,128)(2,1)S(1)} all-to-all(bf16[96,16,128]{2,1,0:T(8,128)(2,1)S(1)} %bitcast.19), channel_id=1, replica_groups=mesh['group'=96,'member'=8] {'group'}, dimensions={0} | all-to-all | bytes 786432 | tf_op jit(solution)/shard_map/all_to_all | solution.py:279
  125.3 0.3 finish.1
  125.6 27.4 %all_to_all.31.got_ref = bf16[96,16,128]{2,1,0:T(8,128)(2,1)S(1)} all-to-all(bf16[96,16,128]{2,1,0:T(8,128)(2,1)S(1)} %get-tuple-element.13), channel_id=1, replica_groups=mesh['group'=96,'member'=8] {'group'}, dimensions={0} | all-to-all | bytes 786432 | tf_op jit(solution)/shard_map/all_to_all | solution.py:279
  153.0 2.2 %spread.1 = (f32[1024,128]{1,0:T(8,128)}, bf16[8,320,128]{2,1,0:T(8,128)(2,1)}) custom-call(bf16[96,16,128]{2,1,0:T(8,128)(2,1)S(1)} %all_to_all.31.got_ref, bf16[192,128]{1,0:T(8,128)(2,1)S(1)} %get-tuple-element.14.cold_ref), custom_call_target="tpu_custom_call" | custom-call | flops 452984832 | bytes 2000000 | tf_op jit(solution)/shard_map/spread/pallas_call | solution.py:194
  155.2 7.8 %all-to-all-start.5 = ((bf16[8,320,128]{2,1,0:T(8,128)(2,1)}), bf16[8,320,128]{2,1,0:T(8,128)(2,1)S(1)}, u32[]{:S(2)}, u32[]{:S(2)}) async-start(bf16[8,320,128]{2,1,0:T(8,128)(2,1)} %get-tuple-element.15), calls=%async_computation.5 | async-start | bytes 1310720 | tf_op jit(solution)/shard_map/all_to_all | solution.py:279
  162.9 0.1 reshape.127
  163.1 1.3 dynamic-slice
  165.0 0.3 dynamic-update-slice
  165.3 10.4 %all-reduce = s32[1536]{0:T(1024)S(1)} all-reduce(s32[1536]{0:T(1024)S(1)} %dynamic-update-slice), channel_id=1, replica_groups=mesh['group'=96,'member'=8] {'member'}, use_global_device_ids=true, to_apply=%add | all-reduce | flops 1536 | bytes 12288
  175.7 0.0 all-to-all-done.5.got_ref
  175.7 1.9 %last.1 = (f32[1024,128]{1,0:T(8,128)}, f32[1024,128]{1,0:T(8,128)}) custom-call(bf16[8,320,128]{2,1,0:T(8,128)(2,1)S(1)} %all-to-all-done.5.got_ref, s32[1,1536]{1,0:T(1,128)S(1)} %reshape.129.to_ref), custom_call_target="tpu_custom_call" | custom-call | flops 402653184 | bytes 2000000 | tf_op jit(solution)/shard_map/last/pallas_call | solution.py:194
  (11 shorter events, 0.1 us)
Async XLA Ops:
  0.6 1.0 copy-start
  0.6 16.7 %copy-start.12 = (s32[1,1,96,2]{2,3,1,0:T(2,128)S(1)}, s32[1,1,96,2]{2,3,1,0:T(2,128)}, u32[]{:S(2)}) copy-start(s32[1,1,96,2]{2,3,1,0:T(2,128)} %param.17) | copy-start | bytes 2308
  0.7 17.0 %copy-start.7 = (bf16[1024,128]{1,0:T(8,128)(2,1)S(1)}, bf16[1024,128]{1,0:T(8,128)(2,1)}, u32[]{:S(2)}) copy-start(bf16[1024,128]{1,0:T(8,128)(2,1)} %param.15) | copy-start | bytes 786436
  0.7 35.7 %copy-start.11 = (bf16[1024]{0:T(1024)(128)(2,1)S(1)}, bf16[1024]{0:T(1024)(128)(2,1)}, u32[]{:S(2)}) copy-start(bf16[1024]{0:T(1024)(128)(2,1)} %param.25) | copy-start | bytes 6148
  0.7 35.7 %copy-start.10 = (f32[2560]{0:T(1024)S(1)}, f32[2560]{0:T(1024)}, u32[]{:S(2)}) copy-start(f32[2560]{0:T(1024)} %param.22) | copy-start | bytes 30724
  0.7 35.7 %copy-start.8 = (s32[256,20]{0,1:T(8,128)S(1)}, s32[256,20]{0,1:T(8,128)}, u32[]{:S(2)}) copy-start(s32[256,20]{0,1:T(8,128)} %param.18) | copy-start | bytes 61444
  0.7 48.6 %copy-start.5 = (f32[1024]{0:T(1024)S(1)}, f32[1024]{0:T(1024)}, u32[]{:S(2)}) copy-start(f32[1024]{0:T(1024)} %param.24) | copy-start | bytes 12292
  0.7 48.6 %copy-start.2 = (bf16[2560,256]{1,0:T(8,128)(2,1)S(1)}, bf16[2560,256]{1,0:T(8,128)(2,1)}, u32[]{:S(2)}) copy-start(bf16[2560,256]{1,0:T(8,128)(2,1)} %v_hbm.1) | copy-start | bytes 3932164
  0.7 48.6 %copy-start.6 = (s32[256]{0:T(256)S(1)}, s32[256]{0:T(256)}, u32[]{:S(2)}) copy-start(s32[256]{0:T(256)} %param.19) | copy-start | bytes 3076
  0.7 48.6 %copy-start.4 = (bf16[1024,128]{1,0:T(8,128)(2,1)S(1)}, bf16[1024,128]{1,0:T(8,128)(2,1)}, u32[]{:S(2)}) copy-start(bf16[1024,128]{1,0:T(8,128)(2,1)} %hot_ref.1) | copy-start | bytes 786436
  3.6 19.1 %all-to-all-start = ((bf16[8,64,128]{2,1,0:T(8,128)(2,1)}), bf16[8,64,128]{2,1,0:T(8,128)(2,1)S(1)}, u32[]{:S(2)}, u32[]{:S(2)}) async-start(bf16[8,64,128]{2,1,0:T(8,128)(2,1)} %bitcast.1), calls=%async_computation | async-start | bytes 262144 | tf_op jit(solution)/shard_map/all_to_all | solution.py:279
  22.7 26.6 %all-to-all-start.1 = ((bf16[96,2,128]{2,1,0:T(2,128)(2,1)}), bf16[96,2,128]{2,1,0:T(2,128)(2,1)S(1)}, u32[]{:S(2)}, u32[]{:S(2)}) async-start(bf16[96,2,128]{2,1,0:T(2,128)(2,1)} %bitcast.4), calls=%async_computation.1 | async-start | bytes 98304 | tf_op jit(solution)/shard_map/all_to_all | solution.py:279
  49.3 2.5 %copy-start.1 = (bf16[2560,1024]{1,0:T(8,128)(2,1)S(1)}, bf16[2560,1024]{1,0:T(8,128)(2,1)}, u32[]{:S(2)}) copy-start(bf16[2560,1024]{1,0:T(8,128)(2,1)} %w_hbm.1) | copy-start | bytes 15728644
  51.8 1.3 copy-start.3
  53.1 35.7 %copy-start.9 = (s32[1,1,8,64]{3,2,1,0:T(8,128)S(1)}, s32[1,1,8,64]{3,2,1,0:T(8,128)}, u32[]{:S(2)}) copy-start(s32[1,1,8,64]{3,2,1,0:T(8,128)} %param.16) | copy-start | bytes 6148
  83.1 13.8 %all-to-all-start.2 = ((bf16[8,192,128]{2,1,0:T(8,128)(2,1)}), bf16[8,192,128]{2,1,0:T(8,128)(2,1)S(1)}, u32[]{:S(2)}, u32[]{:S(2)}) async-start(bf16[8,192,128]{2,1,0:T(8,128)(2,1)} %get-tuple-element.11), calls=%async_computation.2 | async-start | bytes 786432 | tf_op jit(solution)/shard_map/all_to_all | solution.py:279
  155.2 20.5 %all-to-all-start.5 = ((bf16[8,320,128]{2,1,0:T(8,128)(2,1)}), bf16[8,320,128]{2,1,0:T(8,128)(2,1)S(1)}, u32[]{:S(2)}, u32[]{:S(2)}) async-start(bf16[8,320,128]{2,1,0:T(8,128)(2,1)} %get-tuple-element.15), calls=%async_computation.5 | async-start | bytes 1310720 | tf_op jit(solution)/shard_map/all_to_all | solution.py:279

commit v2 on v1

v2 whole, which is shorter than its diff:
```python
import functools

import jax
import jax.numpy as jnp
from jax import lax
from jax.experimental import pallas as pl
from jax.experimental.pallas import tpu as pltpu
from jax.sharding import PartitionSpec as P

F32 = jnp.float32
BF16 = jnp.bfloat16
VMEM = pl.BlockSpec(memory_space=pltpu.VMEM)
HBM = pl.BlockSpec(memory_space=pltpu.HBM)
TILE = 512
LANES = 128
EXTRA = 16


def up(value, step):
    return (value + step - 1) // step * step


def iota(shape, axis):
    return lax.broadcasted_iota(jnp.int32, shape, axis)


def hits(left, right):
    return jnp.where(left == right, 1.0, 0.0).astype(BF16)


def short_hits(left, right):
    met = left.astype(jnp.int16) == right.astype(jnp.int16)
    return jnp.where(met, jnp.ones((), BF16), jnp.zeros((), BF16))


def dot(a, b):
    return jnp.dot(a, b, preferred_element_type=F32)


def dot_nt(a, b):
    return lax.dot_general(a, b, (((1,), (1,)), ((), ())), preferred_element_type=F32)


def column_of(row):
    size = row.shape[1]
    same = iota((size, size), 0) == iota((size, size), 1)
    return jnp.sum(jnp.where(same, row, 0), axis=1, keepdims=True)


def standing(ids_ref):
    fields, batch = ids_ref.shape
    filled = jnp.concatenate([ids_ref[...], jnp.zeros((LANES - fields, batch), jnp.int32)], axis=0)
    return filled.T


def field_column(stood, field):
    return jnp.sum(jnp.where(iota(stood.shape, 1) == field, stood, 0), axis=1, keepdims=True)


def columns(step):
    return pl.ds(pl.multiple_of(step * TILE, TILE), TILE)


def lookup_kernel(hot_ref, warm_ref, ids_ref, out_ref, table, stood_ref):
    rows, width = table.shape
    hot_rows = hot_ref.shape[0]
    table[0:hot_rows, :] = hot_ref[...]
    table[hot_rows:, :] = warm_ref[...]
    batch = ids_ref.shape[1]
    stood_ref[...] = standing(ids_ref)

    @pl.loop(0, out_ref.shape[1] // TILE, unroll=True)
    def _(step):
        pieces = []
        for k in range(TILE // width):
            ids = field_column(stood_ref[...], step * (TILE // width) + k)
            chosen = short_hits(iota((batch, rows), 1), ids)
            pieces.append(dot(chosen, table[...]).astype(BF16))
        out_ref[:, columns(step)] = jnp.concatenate(pieces, axis=1)


def tower_kernel(
    hot_rows, warm_rows,
    found_ref, cold_ref, ids_ref, label_ref, bias_ref, b_in_ref, w_out_ref, v_ref, u_hbm, w_hbm,
    member_ref, cold_out_ref,
    stood_ref, inputs, crossed, d_layer, narrow, preact, total, u_ref, w_ref, sems,
):
    copies = [pltpu.make_async_copy(u_hbm, u_ref, sems.at[0]), pltpu.make_async_copy(w_hbm, w_ref, sems.at[1])]
    for copy in copies:
        copy.start()
    fields, batch = ids_ref.shape
    width = cold_ref.shape[1]
    steps = inputs.shape[1] // TILE
    each = TILE // width
    cold_rows = cold_ref.shape[0]
    slots = hot_rows + warm_rows + cold_rows
    stood_ref[...] = standing(ids_ref)
    narrow[...] = jnp.zeros_like(narrow)

    @pl.loop(0, steps, unroll=True)
    def _(step):
        pieces = []
        for k in range(each):
            ids = field_column(stood_ref[...], step * each + k)
            chosen = short_hits(iota((batch, cold_rows), 1) + (slots - cold_rows), ids)
            pieces.append(dot(chosen, cold_ref[...]))
        fetched = jnp.concatenate(pieces, axis=1)
        part = (found_ref[:, columns(step)].astype(F32) + fetched).astype(BF16)
        inputs[:, columns(step)] = part
        narrow[...] += dot(part, v_ref[columns(step), :])

    low = narrow[...].astype(BF16)
    preact[...] = jnp.zeros_like(preact)
    for copy in copies:
        copy.wait()

    @pl.loop(0, steps, unroll=True)
    def _(step):
        part = inputs[:, columns(step)].astype(F32)
        cross = dot(low, u_ref[:, columns(step)]) + bias_ref[:, columns(step)]
        crossed[:, columns(step)] = cross
        layer_one = (part * cross + part).astype(BF16)
        preact[...] += dot(layer_one, w_ref[columns(step), :])

    pre = preact[...] + b_in_ref[...]
    gate = jax.nn.sigmoid(pre)
    w_out = w_out_ref[...].astype(F32)
    hidden = (pre * gate).astype(BF16).astype(F32)
    logits = jnp.sum(hidden * w_out, axis=1, keepdims=True)
    d_logit = jax.nn.sigmoid(logits) - column_of(label_ref[...].astype(F32))
    d_hidden = (d_logit * w_out * gate * (1.0 + pre * (1.0 - gate))).astype(BF16)
    narrow[...] = jnp.zeros_like(narrow)

    @pl.loop(0, steps, unroll=True)
    def _(step):
        part = inputs[:, columns(step)].astype(F32)
        d_part = dot_nt(d_hidden, w_ref[columns(step), :])
        d_layer[:, columns(step)] = d_part
        d_crossed = (d_part * part).astype(BF16)
        narrow[...] += dot_nt(d_crossed, u_ref[:, columns(step)])

    d_low = narrow[...].astype(BF16)
    total[...] = jnp.zeros_like(total)

    @pl.loop(0, steps, unroll=True)
    def _(step):
        d_in = d_layer[:, columns(step)] * (crossed[:, columns(step)] + 1.0)
        d_in += dot_nt(d_low, v_ref[columns(step), :])
        high = d_in.astype(BF16)
        rest = (d_in - high.astype(F32)).astype(BF16)
        places, values = [], []
        for k in range(each):
            ids = ids_ref[pl.ds(step * each + k, 1), :]
            places.append(short_hits(iota((slots, batch), 0), ids))
            piece = slice(k * width, (k + 1) * width)
            values.append(jnp.concatenate([high[:, piece], rest[:, piece]], axis=1))
        total[...] += dot(jnp.concatenate(places, axis=1), jnp.concatenate(values, axis=0))

    members = member_ref.shape[0]
    hot_each = hot_rows // members
    warm_each = warm_rows // members

    def rows(start, size):
        return (total[start : start + size, :width] + total[start : start + size, width:]).astype(BF16)

    for m in range(members):
        member_ref[m, 0:hot_each, :] = rows(m * hot_each, hot_each)
        member_ref[m, hot_each : hot_each + warm_each, :] = rows(hot_rows + m * warm_each, warm_each)
    cold_out_ref[...] = rows(hot_rows + warm_rows, cold_rows)


def call(kernel, name, out_shape, args, flops, scratch=(), vmem=8, transcendentals=0, apart=0):
    single = isinstance(out_shape, jax.ShapeDtypeStruct)
    return pl.pallas_call(
        kernel,
        name=name,
        out_shape=out_shape,
        in_specs=[VMEM] * (len(args) - apart) + [HBM] * apart,
        out_specs=VMEM if single else tuple(VMEM for _ in out_shape),
        scratch_shapes=list(scratch),
        compiler_params=pltpu.CompilerParams(vmem_limit_bytes=vmem * 2**20),
        cost_estimate=pl.CostEstimate(flops=flops, bytes_accessed=2_000_000, transcendentals=transcendentals),
    )(*args)


def lookup(hot, warm, ids):
    fields, batch = ids.shape
    width = hot.shape[1]
    rows = hot.shape[0] + warm.shape[0]
    return call(
        lookup_kernel, "lookup", jax.ShapeDtypeStruct((batch, fields * width), BF16), (hot, warm, ids),
        4 * batch * fields * rows * width,
        [pltpu.VMEM((rows, width), BF16), pltpu.VMEM((batch, LANES), jnp.int32)], 16,
    )


def tower(found, cold, ids, labels, bias, b_in, w_out, v, u, w, hot_rows, warm_rows, members):
    fields, batch = ids.shape
    width = cold.shape[1]
    wide, rank = v.shape
    hid = w.shape[1]
    slots = hot_rows + warm_rows + cold.shape[0]
    each = (hot_rows + warm_rows) // members
    flops = 2 * batch * wide * (2 * rank + hid) * 2 + 4 * batch * fields * slots * width * 2
    return call(
        functools.partial(tower_kernel, hot_rows, warm_rows),
        "tower",
        (
            jax.ShapeDtypeStruct((members, each, width), BF16),
            jax.ShapeDtypeStruct(cold.shape, BF16),
        ),
        (found, cold, ids, labels, bias, b_in, w_out, v, u, w),
        flops,
        [
            pltpu.VMEM((batch, LANES), jnp.int32),
            pltpu.VMEM((batch, wide), BF16),
            pltpu.VMEM((batch, wide), F32),
            pltpu.VMEM((batch, wide), F32),
            pltpu.VMEM((batch, rank), F32),
            pltpu.VMEM((batch, hid), F32),
            pltpu.VMEM((slots, 2 * width), F32),
            pltpu.VMEM(u.shape, BF16),
            pltpu.VMEM(w.shape, BF16),
            pltpu.SemaphoreType.DMA((2,)),
        ],
        52,
        batch * hid,
        2,
    )


def serve_cold_kernel(table_ref, list_ref, out_ref):
    ccap, groups = list_ref.shape
    shape = (out_ref.shape[0], groups)
    row, group = iota(shape, 0), iota(shape, 1)
    ids = jnp.zeros(shape, jnp.int32)
    for k in range(ccap):
        ids = jnp.where((row // ccap == group) & (row % ccap == k), list_ref[k : k + 1, :], ids)
    ids = jnp.sum(ids, axis=1, keepdims=True)
    out_ref[...] = dot(short_hits(iota((shape[0], table_ref.shape[0]), 1), ids), table_ref[...]).astype(BF16)


def serve_warm_kernel(table_ref, list_ref, out_ref):
    members, wcap = list_ref.shape
    for m in range(members):
        ids = column_of(list_ref[m : m + 1, :])
        out_ref[m] = dot(short_hits(iota((wcap, table_ref.shape[0]), 1), ids), table_ref[...]).astype(BF16)


def owner_kernel(warm_local, chunk, slot, groups, got_ref, cold_ref, list_ref, out_ref):
    out_rows = groups * slot
    members = list_ref.shape[0]
    keep = cold_ref.shape[0]
    keeps = keep // groups
    hot_each = got_ref.shape[0] // members - list_ref.shape[1]
    hot_to = warm_local + iota((1, hot_each), 1)
    to = jnp.concatenate([piece for m in range(members) for piece in (hot_to, list_ref[m : m + 1, :])], axis=1)
    place = iota((out_rows, 1), 0)
    group, at = place // slot, place % slot
    wanted = jnp.where(at < chunk, group * chunk + at, -1)
    cold_wanted = jnp.where((at >= chunk) & (at < chunk + keeps), group * keeps + at - chunk, -1)
    out = dot(hits(wanted, to), got_ref[...])
    out += dot(hits(cold_wanted, iota((out_rows, keep), 1)), cold_ref[...])
    out_ref[...] = out.astype(BF16)


def finish_kernel(chunk, slot, keeps, got_ref, chunk_ref, cold_ref):
    total_rows = got_ref.shape[0]
    groups = total_rows // slot
    rows = up(chunk, 16)
    shape = (rows, total_rows)
    own = jnp.where(iota(shape, 0) < chunk, iota(shape, 0), -1)
    summed = dot(hits(own, iota(shape, 1) % slot), got_ref[...]).astype(BF16)
    place = iota((groups * chunk, rows), 0) % chunk
    chunk_ref[...] = dot(hits(place, iota((groups * chunk, rows), 1)), summed).astype(BF16)
    cold_rows = cold_ref.shape[0]
    row = iota((cold_rows, 1), 0)
    wanted = row % groups * slot + chunk + row // groups
    cold_ref[...] = dot(hits(wanted, iota((cold_rows, total_rows), 1)), got_ref[...]).astype(BF16)


def spread_kernel(got_ref, cold_ref, list_ref, warm_ref, out_ref):
    members = out_ref.shape[0]
    warm_rows, width = warm_ref.shape
    cold_rows = cold_ref.shape[0]
    ccap, groups = list_ref.shape
    hot_each = out_ref.shape[1] - cold_rows - EXTRA
    warm_ref[...] = got_ref[0:warm_rows, :].astype(F32)
    hot = got_ref[warm_rows : warm_rows + hot_each, :]
    places = list_ref[...]
    blank = jnp.zeros((EXTRA, groups), jnp.int32)
    row = iota((EXTRA, groups), 0)
    for k in range(ccap):
        blank = jnp.where(row == 2 * k, places[k : k + 1, :] // 32, blank)
        blank = jnp.where(row == 2 * k + 1, places[k : k + 1, :] % 32, blank)
    code = jnp.concatenate([blank.astype(F32), jnp.zeros((EXTRA, width - groups), F32)], axis=1).astype(BF16)
    for m in range(members):
        out_ref[m, 0:hot_each, :] = hot
        out_ref[m, hot_each : hot_each + cold_rows, :] = cold_ref[...]
        out_ref[m, hot_each + cold_rows :, :] = code


def last_kernel(groups, ccap, got_ref, hot_ref, cold_ref):
    members, each, width = got_ref.shape
    hot_each = hot_ref.shape[0] // members
    cold_local = cold_ref.shape[0]
    last_row = each - EXTRA
    total = jnp.zeros((cold_local, width), F32)
    for m in range(members):
        hot_ref[m * hot_each : (m + 1) * hot_each, :] = got_ref[m, 0:hot_each, :].astype(F32)
        code = got_ref[m, last_row:, :].astype(F32)
        to = [code[2 * k : 2 * k + 1, :groups] * 32.0 + code[2 * k + 1 : 2 * k + 2, :groups] for k in range(ccap)]
        to = jnp.concatenate(to, axis=1).astype(jnp.int32)
        total += dot(short_hits(iota((cold_local, to.shape[1]), 0), to), got_ref[m, hot_each:last_row, :])
    cold_ref[...] = total


def per_device(
    hot_table, warm_table, cold_table, warm_serve, cold_serve, feature_ids, labels,
    cross_v, cross_u, cross_bias, w_in, b_in, w_out,
):
    width = hot_table.shape[1]
    hot_rows = hot_table.shape[0]
    warm_local = warm_table.shape[0]
    cold_local = cold_table.shape[0]
    warm_list = warm_serve[0, 0]
    cold_list = cold_serve[0, 0].T
    ids = feature_ids.T
    members, wcap = warm_list.shape
    ccap, groups = cold_list.shape
    warm_slots = members * wcap
    cold_slots = groups * ccap
    hot_each = hot_rows // members
    chunk = up(up(warm_local + hot_each, groups) // groups, 4)
    slot = up(chunk + ccap, 2)

    def exchange(x, axis):
        return lax.all_to_all(x, axis, split_axis=0, concat_axis=0, tiled=True)

    def exchange_rows(x, tile):
        parts = x.reshape(x.shape[0] // tile, tile, width)
        return exchange(parts, "group").reshape(x.shape)

    def shape(*dims, kind=BF16):
        return jax.ShapeDtypeStruct(dims, kind)

    cold_wanted = call(
        serve_cold_kernel, "serve_cold", shape(cold_slots, width), (cold_table, cold_list),
        2 * cold_slots * cold_local * width,
    )
    cold_fetched = exchange_rows(cold_wanted, ccap)
    warm_wanted = call(
        serve_warm_kernel, "serve_warm", shape(members, wcap, width), (warm_table, warm_list),
        2 * warm_slots * warm_local * width,
    )
    warm_fetched = exchange(warm_wanted, "member").reshape(warm_slots, width)
    found = lookup(hot_table, warm_fetched, ids)
    to_members, cold_part = tower(
        found, cold_fetched, ids, labels.reshape(1, -1),
        cross_bias.reshape(1, -1), b_in.reshape(1, -1), w_out.reshape(1, -1),
        cross_v, cross_u, w_in, hot_rows, warm_slots, members,
    )
    got = exchange(to_members, "member")
    to_groups = call(
        functools.partial(owner_kernel, warm_local, chunk, slot, groups),
        "owner",
        shape(groups * slot, width),
        (got.reshape(-1, width), cold_part, warm_list),
        2 * groups * slot * width * (hot_rows + warm_slots + cold_slots),
        vmem=16,
    )
    summands = exchange_rows(to_groups, 2)
    my_chunk, my_cold = call(
        functools.partial(finish_kernel, chunk, slot, ccap),
        "finish",
        (shape(groups * chunk, width), shape(cold_slots, width)),
        (summands,),
        2 * groups * slot * width * cold_slots,
    )
    chunks = exchange_rows(my_chunk, 4)
    warm_grad, to_all = call(
        spread_kernel,
        "spread",
        (shape(warm_local, width, kind=F32), shape(members, hot_each + cold_slots + EXTRA, width)),
        (chunks, my_cold, cold_list),
        2 * groups * slot * width,
    )
    last = exchange(to_all, "member")
    hot_grad, cold_grad = call(
        functools.partial(last_kernel, groups, ccap),
        "last",
        (shape(hot_rows, width, kind=F32), shape(cold_local, width, kind=F32)),
        (last,),
        2 * cold_local * members * cold_slots * width,
    )
    return hot_grad, warm_grad, cold_grad


def solution(mesh):
    placed = (
        P(),
        P("member", None),
        P("group", None),
        P("group", "member", None, None),
        P("group", "member", None, None),
        P(("group", "member"), None),
        P(("group", "member")),
        P(),
        P(),
        P(),
        P(),
        P(),
        P(),
    )
    return jax.shard_map(
        per_device,
        mesh=mesh,
        in_specs=placed,
        out_specs=(P(), P("member", None), P("group", None)),
        check_vma=False,
    )
```

time: 178 us -> 158 us (0.89)
  blocking collectives: 64.5 us -> 82.6 us
  waiting for transfers between devices: 24.3 us -> 7.85 us
  starting transfers between devices: 41 us -> 27.7 us
  local copies, waits for them, and re-layouts: 10.2 us -> 6.36 us
  Pallas kernels: 36 us -> 32.2 us
    pallas_call x1 -> x0, Pallas kernels: 29.9 us -> none  [tower(): pl.pallas_call(tower_kernel, name='tower', out_shape=(jax.ShapeDtypeStruc...]
    all_to_all x2 -> x4, blocking collectives: 54.1 us -> 82.6 us  [exchange(): return lax.all_to_all(x, axis, split_axis=0, concat_axis=0, tiled=True)]
    pallas_call x4 -> x8, Pallas kernels: 6.06 us -> 32.2 us  [call(): pl.pallas_call(kernel, name=name, out_shape=out_shape, in_specs=[VMEM] *...]
    all_to_all x4 -> x2, waiting for transfers between devices: 24.3 us -> 7.85 us  [exchange(): return lax.all_to_all(x, axis, split_axis=0, concat_axis=0, tiled=True)]
    all_to_all x4 -> x2, starting transfers between devices: 41 us -> 27.7 us  [exchange(): return lax.all_to_all(x, axis, split_axis=0, concat_axis=0, tiled=True)]
    unnamed x1 -> x0, blocking collectives: 10.4 us -> none
    gather x2 -> x0, local copies, waits for them, and re-layouts: 3.31 us -> none  [the longest x1 1.92 us: per_device(): warm_table[warm_list.reshape(-1)].reshape(members, wcap, width)]
    unnamed x33 -> x22, local copies, waits for them, and re-layouts: 5.77 us -> 4.96 us
  transfers between devices with their start and end apart: 4 -> 2, of which waited for: 3 -> 2; matrix products, arithmetic and copies ran while one was open for 2% -> 1% of each run, Pallas kernels for 0% -> 3%
where the time goes in v2:
time: 158 us; the launch traced here: 157 us
  blocking collectives  82.6 us (52%)
  Pallas kernels  32.2 us (20%)
  starting transfers between devices  27.7 us (18%)
  waiting for transfers between devices  7.85 us (5%)
  local copies, waits for them, and re-layouts  6.36 us (4%)
    all_to_all x4, blocking collectives, exchange(): return lax.all_to_all(x, axis, split_axis=0, concat_axis=0, tiled=True)  82.6 us
    pallas_call x8, Pallas kernels, call(): pl.pallas_call(kernel, name=name, out_shape=out_shape, in_specs=[VMEM] *...  32.2 us
    all_to_all x2, starting transfers between devices, exchange(): return lax.all_to_all(x, axis, split_axis=0, concat_axis=0, tiled=True)  27.7 us
    all_to_all x2, waiting for transfers between devices, exchange(): return lax.all_to_all(x, axis, split_axis=0, concat_axis=0, tiled=True)  7.85 us
    unnamed x22, local copies, waits for them, and re-layouts  4.96 us
  transfers between devices with their start and end apart: 2, of which 2 were waited for; matrix products, arithmetic and copies ran while one was open for 1% of the time, Pallas kernels for 3%

profile of v2, /device:TPU:1, one launch (start us, length us, event | category | flops | bytes accessed | tf_op | source)
XLA Modules:
  0.0 157.3 jit_solution(6183810517065889375)
XLA Ops:
  0.6 0.0 copy-start.3
  0.6 0.9 copy-done.3
  1.6 0.0 copy-start.8
  1.6 0.7 copy-done.8
  2.3 1.2 serve_warm.1
  3.4 13.8 %all-to-all-start = ((bf16[8,64,128]{2,1,0:T(8,128)(2,1)}), bf16[8,64,128]{2,1,0:T(8,128)(2,1)S(1)}, u32[]{:S(2)}, u32[]{:S(2)}) async-start(bf16[8,64,128]{2,1,0:T(8,128)(2,1)} %serve_warm.1), calls=%async_computation | async-start | bytes 262144 | tf_op jit(solution)/shard_map/all_to_all | solution.py:338
  17.2 0.7 reshape.48.w_out_ref
  17.9 0.7 reshape.46.bias_ref
  18.6 0.0 copy-start
  18.6 0.9 copy-done
  19.6 0.0 copy-start.1
  19.6 0.7 copy-done.1
  20.2 1.0 serve_cold.1
  21.2 1.3 all-to-all-done
  22.5 13.9 %all-to-all-start.1 = ((bf16[96,2,128]{2,1,0:T(2,128)(2,1)}), bf16[96,2,128]{2,1,0:T(2,128)(2,1)S(1)}, u32[]{:S(2)}, u32[]{:S(2)}) async-start(bf16[96,2,128]{2,1,0:T(2,128)(2,1)} %bitcast.5), calls=%async_computation.1 | async-start | bytes 98304 | tf_op jit(solution)/shard_map/all_to_all | solution.py:338
  36.4 0.0 copy-start.4
  36.4 0.9 copy-done.4
  37.4 0.0 copy-start.5
  37.4 0.7 copy-done.5
  38.1 0.0 copy-start.6
  38.1 0.0 copy-start.7
  38.1 0.0 copy-start.10
  38.1 4.5 %lookup.1.found_ref = bf16[256,2560]{1,0:T(8,128)(2,1)S(1)} custom-call(bf16[1024,128]{1,0:T(8,128)(2,1)S(1)} %copy-done.4, bf16[512,128]{1,0:T(8,128)(2,1)S(1)} %bitcast.20, s32[20,256]{1,0:T(8,128)S(1)} %bitcast.24), custom_call_target="tpu_custom_call" | custom-call | flops 4026531840 | bytes 2000000 | tf_op jit(solution)/shard_map/lookup/pallas_call | solution.py:174
  42.6 6.5 %all-to-all-done.1 = bf16[96,2,128]{2,1,0:T(2,128)(2,1)S(1)} async-done(((bf16[96,2,128]{2,1,0:T(2,128)(2,1)}), bf16[96,2,128]{2,1,0:T(2,128)(2,1)S(1)}, u32[]{:S(2)}, u32[]{:S(2)}) %all-to-all-start.1) | async-done | bytes 49184 | tf_op jit(solution)/shard_map/all_to_all | solution.py:338
  49.1 0.0 copy-done.6
  49.1 0.0 copy-done.7
  49.1 0.0 copy-done.10
  49.1 0.0 copy-start.9
  49.2 19.9 %tower.1 = (bf16[8,192,128]{2,1,0:T(8,128)(2,1)S(1)}, bf16[192,128]{1,0:T(8,128)(2,1)S(1)}) custom-call(bf16[256,2560]{1,0:T(8,128)(2,1)S(1)} %lookup.1.found_ref, bf16[192,128]{1,0:T(8,128)(2,1)S(1)} %bitcast.21, s32[20,256]{1,0:T(8,128)S(1)} %bitcast.25, s32[1,256]{1,0:T(1,128)S(1)} %bitcast.29, f32[1,2560]{1,0:T(1,128)S(1)} %reshape.46.bias_ref, ...), custom_call_target="tpu_custom_call" | custom-call | flops 13086228480 | bytes 2000000 | tf_op jit(solution)/shard_map/tower/pallas_call | solution.py:174
  69.1 12.8 %all_to_all.30 = bf16[8,192,128]{2,1,0:T(8,128)(2,1)S(1)} all-to-all(bf16[8,192,128]{2,1,0:T(8,128)(2,1)S(1)} %get-tuple-element.11), channel_id=1, replica_groups=mesh['group'=96,'member'=8] {'member'}, dimensions={0} | all-to-all | bytes 786432 | tf_op jit(solution)/shard_map/all_to_all | solution.py:338
  81.9 0.0 copy-done.9
  81.9 1.9 %owner.1 = bf16[1344,128]{1,0:T(8,128)(2,1)S(1)} custom-call(bf16[1536,128]{1,0:T(8,128)(2,1)S(1)} %bitcast.17, bf16[192,128]{1,0:T(8,128)(2,1)S(1)} %get-tuple-element.12.cold_ref, s32[8,64]{1,0:T(8,128)S(1)} %bitcast.28), custom_call_target="tpu_custom_call" | custom-call | flops 594542592 | bytes 2000000 | tf_op jit(solution)/shard_map/owner/pallas_call | solution.py:174
  83.8 0.0 copy-start.2
  83.8 27.2 %all_to_all.31 = bf16[672,2,128]{2,1,0:T(2,128)(2,1)S(1)} all-to-all(bf16[672,2,128]{2,1,0:T(2,128)(2,1)S(1)} %bitcast.18), channel_id=1, replica_groups=mesh['group'=96,'member'=8] {'group'}, dimensions={0} | all-to-all | bytes 688128 | tf_op jit(solution)/shard_map/all_to_all | solution.py:338
  111.1 0.6 finish.1
  111.7 25.0 %all_to_all.32 = bf16[288,4,128]{2,1,0:T(4,128)(2,1)S(1)} all-to-all(bf16[288,4,128]{2,1,0:T(4,128)(2,1)S(1)} %bitcast.19), channel_id=1, replica_groups=mesh['group'=96,'member'=8] {'group'}, dimensions={0} | all-to-all | bytes 589824 | tf_op jit(solution)/shard_map/all_to_all | solution.py:338
  136.7 0.0 copy-done.2
  136.7 0.9 spread.1
  137.6 17.5 %all_to_all.33.got_ref = bf16[8,336,128]{2,1,0:T(8,128)(2,1)S(1)} all-to-all(bf16[8,336,128]{2,1,0:T(8,128)(2,1)S(1)} %get-tuple-element.15), channel_id=1, replica_groups=mesh['group'=96,'member'=8] {'member'}, dimensions={0} | all-to-all | bytes 1376256 | tf_op jit(solution)/shard_map/all_to_all | solution.py:338
  155.1 2.2 %last.1 = (f32[1024,128]{1,0:T(8,128)}, f32[1024,128]{1,0:T(8,128)}) custom-call(bf16[8,336,128]{2,1,0:T(8,128)(2,1)S(1)} %all_to_all.33.got_ref), custom_call_target="tpu_custom_call" | custom-call | flops 402653184 | bytes 2000000 | tf_op jit(solution)/shard_map/last/pallas_call | solution.py:174
Async XLA Ops:
  0.6 1.0 copy-start.3
  1.6 0.7 copy-start.8
  3.4 19.1 %all-to-all-start = ((bf16[8,64,128]{2,1,0:T(8,128)(2,1)}), bf16[8,64,128]{2,1,0:T(8,128)(2,1)S(1)}, u32[]{:S(2)}, u32[]{:S(2)}) async-start(bf16[8,64,128]{2,1,0:T(8,128)(2,1)} %serve_warm.1), calls=%async_computation | async-start | bytes 262144 | tf_op jit(solution)/shard_map/all_to_all | solution.py:338
  18.6 0.9 copy-start
  19.6 0.7 copy-start.1
  22.5 26.6 %all-to-all-start.1 = ((bf16[96,2,128]{2,1,0:T(2,128)(2,1)}), bf16[96,2,128]{2,1,0:T(2,128)(2,1)S(1)}, u32[]{:S(2)}, u32[]{:S(2)}) async-start(bf16[96,2,128]{2,1,0:T(2,128)(2,1)} %bitcast.5), calls=%async_computation.1 | async-start | bytes 98304 | tf_op jit(solution)/shard_map/all_to_all | solution.py:338
  36.4 1.0 copy-start.4
  37.4 0.7 copy-start.5
  38.1 11.0 %copy-start.6 = (s32[256,20]{0,1:T(8,128)S(1)}, s32[256,20]{0,1:T(8,128)}, u32[]{:S(2)}) copy-start(s32[256,20]{0,1:T(8,128)} %param.18) | copy-start | bytes 61444
  38.1 11.0 %copy-start.7 = (f32[1024]{0:T(1024)S(1)}, f32[1024]{0:T(1024)}, u32[]{:S(2)}) copy-start(f32[1024]{0:T(1024)} %param.24) | copy-start | bytes 12292
  38.1 11.0 %copy-start.10 = (s32[256]{0:T(256)S(1)}, s32[256]{0:T(256)}, u32[]{:S(2)}) copy-start(s32[256]{0:T(256)} %param.19) | copy-start | bytes 3076
  49.1 32.8 %copy-start.9 = (s32[1,1,8,64]{3,2,1,0:T(8,128)S(1)}, s32[1,1,8,64]{3,2,1,0:T(8,128)}, u32[]{:S(2)}) copy-start(s32[1,1,8,64]{3,2,1,0:T(8,128)} %param.16) | copy-start | bytes 6148
  83.8 52.9 %copy-start.2 = (s32[1,1,96,2]{2,3,1,0:T(2,128)S(1)}, s32[1,1,96,2]{2,3,1,0:T(2,128)}, u32[]{:S(2)}) copy-start(s32[1,1,96,2]{2,3,1,0:T(2,128)} %param.17) | copy-start | bytes 2308

commit v3 on v2

--- a/solution.py
+++ b/solution.py
@@ -58,7 +58,7 @@
 
 
 def columns(step):
-    return pl.ds(pl.multiple_of(step * TILE, TILE), TILE)
+    return pl.ds(step * TILE if isinstance(step, int) else pl.multiple_of(step * TILE, TILE), TILE)
 
 
 def lookup_kernel(hot_ref, warm_ref, ids_ref, out_ref, table, stood_ref):
@@ -81,12 +81,17 @@
 
 def tower_kernel(
     hot_rows, warm_rows,
-    found_ref, cold_ref, ids_ref, label_ref, bias_ref, b_in_ref, w_out_ref, v_ref, u_hbm, w_hbm,
+    found_ref, cold_ref, ids_ref, label_ref, bias_ref, b_in_ref, w_out_ref, v_hbm, u_hbm, w_hbm,
     member_ref, cold_out_ref,
-    stood_ref, inputs, crossed, d_layer, narrow, preact, total, u_ref, w_ref, sems,
+    stood_ref, inputs, crossed, d_layer, narrow, preact, total, v_ref, u_ref, w_ref, sems,
 ):
-    copies = [pltpu.make_async_copy(u_hbm, u_ref, sems.at[0]), pltpu.make_async_copy(w_hbm, w_ref, sems.at[1])]
-    for copy in copies:
+    v_copy = pltpu.make_async_copy(v_hbm, v_ref, sems.at[0])
+    u_copy = pltpu.make_async_copy(u_hbm, u_ref, sems.at[1])
+    w_copies = [
+        pltpu.make_async_copy(w_hbm.at[pl.ds(at, TILE), :], w_ref.at[pl.ds(at, TILE), :], sems.at[2 + at // TILE])
+        for at in range(0, w_ref.shape[0], TILE)
+    ]
+    for copy in (v_copy, u_copy, *w_copies):
         copy.start()
     fields, batch = ids_ref.shape
     width = cold_ref.shape[1]
@@ -96,6 +101,7 @@
     slots = hot_rows + warm_rows + cold_rows
     stood_ref[...] = standing(ids_ref)
     narrow[...] = jnp.zeros_like(narrow)
+    v_copy.wait()
 
     @pl.loop(0, steps, unroll=True)
     def _(step):
@@ -111,11 +117,10 @@
 
     low = narrow[...].astype(BF16)
     preact[...] = jnp.zeros_like(preact)
-    for copy in copies:
-        copy.wait()
-
-    @pl.loop(0, steps, unroll=True)
-    def _(step):
+    u_copy.wait()
+
+    for step in range(steps):
+        w_copies[step].wait()
         part = inputs[:, columns(step)].astype(F32)
         cross = dot(low, u_ref[:, columns(step)]) + bias_ref[:, columns(step)]
         crossed[:, columns(step)] = cross
@@ -147,21 +152,20 @@
         d_in = d_layer[:, columns(step)] * (crossed[:, columns(step)] + 1.0)
         d_in += dot_nt(d_low, v_ref[columns(step), :])
         high = d_in.astype(BF16)
-        rest = (d_in - high.astype(F32)).astype(BF16)
-        places, values = [], []
         for k in range(each):
-            ids = ids_ref[pl.ds(step * each + k, 1), :]
-            places.append(short_hits(iota((slots, batch), 0), ids))
+            ids = field_column(stood_ref[...], step * each + k)
             piece = slice(k * width, (k + 1) * width)
-            values.append(jnp.concatenate([high[:, piece], rest[:, piece]], axis=1))
-        total[...] += dot(jnp.concatenate(places, axis=1), jnp.concatenate(values, axis=0))
+            value = high[:, piece]
+            total[...] += lax.dot_general(value, short_hits(iota((batch, slots), 1), ids), (((0,), (0,)), ((), ())), preferred_element_type=F32)
 
     members = member_ref.shape[0]
     hot_each = hot_rows // members
     warm_each = warm_rows // members
 
+    turned = total[...].T
+
     def rows(start, size):
-        return (total[start : start + size, :width] + total[start : start + size, width:]).astype(BF16)
+        return turned[start : start + size, :].astype(BF16)
 
     for m in range(members):
         member_ref[m, 0:hot_each, :] = rows(m * hot_each, hot_each)
@@ -218,14 +222,15 @@
             pltpu.VMEM((batch, wide), F32),
             pltpu.VMEM((batch, rank), F32),
             pltpu.VMEM((batch, hid), F32),
-            pltpu.VMEM((slots, 2 * width), F32),
+            pltpu.VMEM((width, slots), F32),
+            pltpu.VMEM(v.shape, BF16),
             pltpu.VMEM(u.shape, BF16),
             pltpu.VMEM(w.shape, BF16),
-            pltpu.SemaphoreType.DMA((2,)),
+            pltpu.SemaphoreType.DMA((2 + wide // TILE,)),
         ],
         52,
         batch * hid,
-        2,
+        3,
     )
 
 
@@ -280,13 +285,13 @@
 
 
 def spread_kernel(got_ref, cold_ref, list_ref, warm_ref, out_ref):
-    members = out_ref.shape[0]
     warm_rows, width = warm_ref.shape
     cold_rows = cold_ref.shape[0]
     ccap, groups = list_ref.shape
-    hot_each = out_ref.shape[1] - cold_rows - EXTRA
+    hot_each = out_ref.shape[0] - cold_rows - EXTRA
     warm_ref[...] = got_ref[0:warm_rows, :].astype(F32)
-    hot = got_ref[warm_rows : warm_rows + hot_each, :]
+    out_ref[0:hot_each, :] = got_ref[warm_rows : warm_rows + hot_each, :]
+    out_ref[hot_each : hot_each + cold_rows, :] = cold_ref[...]
     places = list_ref[...]
     blank = jnp.zeros((EXTRA, groups), jnp.int32)
     row = iota((EXTRA, groups), 0)
@@ -294,10 +299,7 @@
         blank = jnp.where(row == 2 * k, places[k : k + 1, :] // 32, blank)
         blank = jnp.where(row == 2 * k + 1, places[k : k + 1, :] % 32, blank)
     code = jnp.concatenate([blank.astype(F32), jnp.zeros((EXTRA, width - groups), F32)], axis=1).astype(BF16)
-    for m in range(members):
-        out_ref[m, 0:hot_each, :] = hot
-        out_ref[m, hot_each : hot_each + cold_rows, :] = cold_ref[...]
-        out_ref[m, hot_each + cold_rows :, :] = code
+    out_ref[hot_each + cold_rows :, :] = code
 
 
 def last_kernel(groups, ccap, got_ref, hot_ref, cold_ref):
@@ -381,11 +383,11 @@
     warm_grad, to_all = call(
         spread_kernel,
         "spread",
-        (shape(warm_local, width, kind=F32), shape(members, hot_each + cold_slots + EXTRA, width)),
+        (shape(warm_local, width, kind=F32), shape(hot_each + cold_slots + EXTRA, width)),
         (chunks, my_cold, cold_list),
         2 * groups * slot * width,
     )
-    last = exchange(to_all, "member")
+    last = lax.all_gather(to_all, "member", axis=0)
     hot_grad, cold_grad = call(
         functools.partial(last_kernel, groups, ccap),
         "last",

time: 158 us -> 150 us (0.949)
  Pallas kernels: 32.2 us -> 24.4 us
    all_to_all x4 -> x3, blocking collectives: 82.6 us -> 65.1 us  [exchange(): return lax.all_to_all(x, axis, split_axis=0, concat_axis=0, tiled=True)]
    all_gather x0 -> x1, blocking collectives: none -> 16.9 us  [per_device(): last = lax.all_gather(to_all, 'member', axis=0)]
    pallas_call x8, Pallas kernels: 32.2 us -> 24.4 us  [call(): pl.pallas_call(kernel, name=name, out_shape=out_shape, in_specs=[VMEM] *...]
  transfers between devices with their start and end apart: 2 -> 2, of which waited for: 2 -> 2; matrix products, arithmetic and copies ran while one was open for 1% -> 1% of each run, Pallas kernels for 3% -> 4%
where the time goes in v3:
time: 150 us; the launch traced here: 149 us
  blocking collectives  82 us (55%)
  starting transfers between devices  27.7 us (18%)
  Pallas kernels  24.4 us (16%)
  waiting for transfers between devices  7.85 us (5%)
  local copies, waits for them, and re-layouts  6.36 us (4%)
    all_to_all x3, blocking collectives, exchange(): return lax.all_to_all(x, axis, split_axis=0, concat_axis=0, tiled=True)  65.1 us
    all_to_all x2, starting transfers between devices, exchange(): return lax.all_to_all(x, axis, split_axis=0, concat_axis=0, tiled=True)  27.7 us
    pallas_call x8, Pallas kernels, call(): pl.pallas_call(kernel, name=name, out_shape=out_shape, in_specs=[VMEM] *...  24.4 us
    all_gather x1, blocking collectives, per_device(): last = lax.all_gather(to_all, 'member', axis=0)  16.9 us
    all_to_all x2, waiting for transfers between devices, exchange(): return lax.all_to_all(x, axis, split_axis=0, concat_axis=0, tiled=True)  7.85 us
    unnamed x22, local copies, waits for them, and re-layouts  4.96 us
  transfers between devices with their start and end apart: 2, of which 2 were waited for; matrix products, arithmetic and copies ran while one was open for 1% of the time, Pallas kernels for 4%

profile of v3, /device:TPU:1, one launch (start us, length us, event | category | flops | bytes accessed | tf_op | source)
XLA Modules:
  0.0 149.0 jit_solution(14540145118172374868)
XLA Ops:
  0.6 0.0 copy-start.3
  0.6 0.9 copy-done.3
  1.6 0.0 copy-start.8
  1.6 0.7 copy-done.8
  2.3 1.2 serve_warm.1
  3.4 13.8 %all-to-all-start = ((bf16[8,64,128]{2,1,0:T(8,128)(2,1)}), bf16[8,64,128]{2,1,0:T(8,128)(2,1)S(1)}, u32[]{:S(2)}, u32[]{:S(2)}) async-start(bf16[8,64,128]{2,1,0:T(8,128)(2,1)} %serve_warm.1), calls=%async_computation | async-start | bytes 262144 | tf_op jit(solution)/shard_map/all_to_all | solution.py:340
  17.2 0.7 reshape.48.w_out_ref
  17.9 0.7 reshape.46.bias_ref
  18.6 0.0 copy-start
  18.6 0.9 copy-done
  19.6 0.0 copy-start.1
  19.6 0.7 copy-done.1
  20.2 1.0 serve_cold.1
  21.2 1.3 all-to-all-done
  22.5 13.9 %all-to-all-start.1 = ((bf16[96,2,128]{2,1,0:T(2,128)(2,1)}), bf16[96,2,128]{2,1,0:T(2,128)(2,1)S(1)}, u32[]{:S(2)}, u32[]{:S(2)}) async-start(bf16[96,2,128]{2,1,0:T(2,128)(2,1)} %bitcast.5), calls=%async_computation.1 | async-start | bytes 98304 | tf_op jit(solution)/shard_map/all_to_all | solution.py:340
  36.4 0.0 copy-start.4
  36.4 0.9 copy-done.4
  37.4 0.0 copy-start.5
  37.4 0.7 copy-done.5
  38.1 0.0 copy-start.6
  38.1 0.0 copy-start.7
  38.1 0.0 copy-start.10
  38.1 4.5 %lookup.1.found_ref = bf16[256,2560]{1,0:T(8,128)(2,1)S(1)} custom-call(bf16[1024,128]{1,0:T(8,128)(2,1)S(1)} %copy-done.4, bf16[512,128]{1,0:T(8,128)(2,1)S(1)} %bitcast.22, s32[20,256]{1,0:T(8,128)S(1)} %bitcast.26), custom_call_target="tpu_custom_call" | custom-call | flops 4026531840 | bytes 2000000 | tf_op jit(solution)/shard_map/lookup/pallas_call | solution.py:178
  42.6 6.5 %all-to-all-done.1 = bf16[96,2,128]{2,1,0:T(2,128)(2,1)S(1)} async-done(((bf16[96,2,128]{2,1,0:T(2,128)(2,1)}), bf16[96,2,128]{2,1,0:T(2,128)(2,1)S(1)}, u32[]{:S(2)}, u32[]{:S(2)}) %all-to-all-start.1) | async-done | bytes 49184 | tf_op jit(solution)/shard_map/all_to_all | solution.py:340
  49.1 0.0 copy-done.6
  49.1 0.0 copy-done.7
  49.1 0.0 copy-done.10
  49.1 0.0 copy-start.9
  49.2 12.2 %tower.1 = (bf16[8,192,128]{2,1,0:T(8,128)(2,1)S(1)}, bf16[192,128]{1,0:T(8,128)(2,1)S(1)}) custom-call(bf16[256,2560]{1,0:T(8,128)(2,1)S(1)} %lookup.1.found_ref, bf16[192,128]{1,0:T(8,128)(2,1)S(1)} %bitcast.23, s32[20,256]{1,0:T(8,128)S(1)} %bitcast.27, s32[1,256]{1,0:T(1,128)S(1)} %bitcast.31, f32[1,2560]{1,0:T(1,128)S(1)} %reshape.46.bias_ref, ...), custom_call_target="tpu_custom_call" | custom-call | flops 13086228480 | bytes 2000000 | tf_op jit(solution)/shard_map/tower/pallas_call | solution.py:178
  61.4 12.8 %all_to_all.25 = bf16[8,192,128]{2,1,0:T(8,128)(2,1)S(1)} all-to-all(bf16[8,192,128]{2,1,0:T(8,128)(2,1)S(1)} %get-tuple-element.11), channel_id=1, replica_groups=mesh['group'=96,'member'=8] {'member'}, dimensions={0} | all-to-all | bytes 786432 | tf_op jit(solution)/shard_map/all_to_all | solution.py:340
  74.2 0.0 copy-done.9
  74.2 1.9 %owner.1 = bf16[1344,128]{1,0:T(8,128)(2,1)S(1)} custom-call(bf16[1536,128]{1,0:T(8,128)(2,1)S(1)} %bitcast.19, bf16[192,128]{1,0:T(8,128)(2,1)S(1)} %get-tuple-element.12.cold_ref, s32[8,64]{1,0:T(8,128)S(1)} %bitcast.30), custom_call_target="tpu_custom_call" | custom-call | flops 594542592 | bytes 2000000 | tf_op jit(solution)/shard_map/owner/pallas_call | solution.py:178
  76.1 0.0 copy-start.2
  76.1 27.2 %all_to_all.26 = bf16[672,2,128]{2,1,0:T(2,128)(2,1)S(1)} all-to-all(bf16[672,2,128]{2,1,0:T(2,128)(2,1)S(1)} %bitcast.20), channel_id=1, replica_groups=mesh['group'=96,'member'=8] {'group'}, dimensions={0} | all-to-all | bytes 688128 | tf_op jit(solution)/shard_map/all_to_all | solution.py:340
  103.3 0.6 finish.1
  104.0 25.0 %all_to_all.27 = bf16[288,4,128]{2,1,0:T(4,128)(2,1)S(1)} all-to-all(bf16[288,4,128]{2,1,0:T(4,128)(2,1)S(1)} %bitcast.21), channel_id=1, replica_groups=mesh['group'=96,'member'=8] {'group'}, dimensions={0} | all-to-all | bytes 589824 | tf_op jit(solution)/shard_map/all_to_all | solution.py:340
  129.0 0.0 copy-done.2
  129.0 0.8 spread.1
  129.8 16.9 %all-gather = bf16[2688,128]{1,0:T(8,128)(2,1)S(1)} all-gather(bf16[336,128]{1,0:T(8,128)(2,1)S(1)} %get-tuple-element.15), channel_id=2, replica_groups=mesh['group'=96,'member'=8] {'member'}, dimensions={0}, use_global_device_ids=true | all-gather | bytes 774144 | tf_op jit(solution)/shard_map/all_gather | solution.py:390
  146.8 2.2 %last.1 = (f32[1024,128]{1,0:T(8,128)}, f32[1024,128]{1,0:T(8,128)}) custom-call(bf16[8,336,128]{2,1,0:T(8,128)(2,1)S(1)} %bitcast.18), custom_call_target="tpu_custom_call" | custom-call | flops 402653184 | bytes 2000000 | tf_op jit(solution)/shard_map/last/pallas_call | solution.py:178
Async XLA Ops:
  0.6 1.0 copy-start.3
  1.6 0.7 copy-start.8
  3.4 19.1 %all-to-all-start = ((bf16[8,64,128]{2,1,0:T(8,128)(2,1)}), bf16[8,64,128]{2,1,0:T(8,128)(2,1)S(1)}, u32[]{:S(2)}, u32[]{:S(2)}) async-start(bf16[8,64,128]{2,1,0:T(8,128)(2,1)} %serve_warm.1), calls=%async_computation | async-start | bytes 262144 | tf_op jit(solution)/shard_map/all_to_all | solution.py:340
  18.6 0.9 copy-start
  19.6 0.7 copy-start.1
  22.5 26.6 %all-to-all-start.1 = ((bf16[96,2,128]{2,1,0:T(2,128)(2,1)}), bf16[96,2,128]{2,1,0:T(2,128)(2,1)S(1)}, u32[]{:S(2)}, u32[]{:S(2)}) async-start(bf16[96,2,128]{2,1,0:T(2,128)(2,1)} %bitcast.5), calls=%async_computation.1 | async-start | bytes 98304 | tf_op jit(solution)/shard_map/all_to_all | solution.py:340
  36.4 1.0 copy-start.4
  37.4 0.7 copy-start.5
  38.1 11.0 %copy-start.6 = (s32[256,20]{0,1:T(8,128)S(1)}, s32[256,20]{0,1:T(8,128)}, u32[]{:S(2)}) copy-start(s32[256,20]{0,1:T(8,128)} %param.18) | copy-start | bytes 61444
  38.1 11.0 %copy-start.7 = (f32[1024]{0:T(1024)S(1)}, f32[1024]{0:T(1024)}, u32[]{:S(2)}) copy-start(f32[1024]{0:T(1024)} %param.24) | copy-start | bytes 12292
  38.1 11.0 %copy-start.10 = (s32[256]{0:T(256)S(1)}, s32[256]{0:T(256)}, u32[]{:S(2)}) copy-start(s32[256]{0:T(256)} %param.19) | copy-start | bytes 3076
  49.1 25.1 %copy-start.9 = (s32[1,1,8,64]{3,2,1,0:T(8,128)S(1)}, s32[1,1,8,64]{3,2,1,0:T(8,128)}, u32[]{:S(2)}) copy-start(s32[1,1,8,64]{3,2,1,0:T(8,128)} %param.16) | copy-start | bytes 6148
  76.1 52.9 %copy-start.2 = (s32[1,1,96,2]{2,3,1,0:T(2,128)S(1)}, s32[1,1,96,2]{2,3,1,0:T(2,128)}, u32[]{:S(2)}) copy-start(s32[1,1,96,2]{2,3,1,0:T(2,128)} %param.17) | copy-start | bytes 2308

commit v4 on v3

--- a/solution.py
+++ b/solution.py
@@ -269,7 +269,7 @@
     out_ref[...] = out.astype(BF16)
 
 
-def finish_kernel(chunk, slot, keeps, got_ref, chunk_ref, cold_ref):
+def finish_kernel(chunk, slot, got_ref, list_ref, chunk_ref, cold_ref):
     total_rows = got_ref.shape[0]
     groups = total_rows // slot
     rows = up(chunk, 16)
@@ -278,43 +278,42 @@
     summed = dot(hits(own, iota(shape, 1) % slot), got_ref[...]).astype(BF16)
     place = iota((groups * chunk, rows), 0) % chunk
     chunk_ref[...] = dot(hits(place, iota((groups * chunk, rows), 1)), summed).astype(BF16)
-    cold_rows = cold_ref.shape[0]
+    ccap = list_ref.shape[0]
+    cold_rows, width = groups * ccap, cold_ref.shape[1]
     row = iota((cold_rows, 1), 0)
     wanted = row % groups * slot + chunk + row // groups
-    cold_ref[...] = dot(hits(wanted, iota((cold_rows, total_rows), 1)), got_ref[...]).astype(BF16)
-
-
-def spread_kernel(got_ref, cold_ref, list_ref, warm_ref, out_ref):
-    warm_rows, width = warm_ref.shape
-    cold_rows = cold_ref.shape[0]
-    ccap, groups = list_ref.shape
-    hot_each = out_ref.shape[0] - cold_rows - EXTRA
-    warm_ref[...] = got_ref[0:warm_rows, :].astype(F32)
-    out_ref[0:hot_each, :] = got_ref[warm_rows : warm_rows + hot_each, :]
-    out_ref[hot_each : hot_each + cold_rows, :] = cold_ref[...]
-    places = list_ref[...]
-    blank = jnp.zeros((EXTRA, groups), jnp.int32)
+    picked = dot(hits(wanted, iota((cold_rows, total_rows), 1)), got_ref[...])
+    cold_ref[0:cold_rows, :] = picked.astype(BF16)
+    code = jnp.zeros((EXTRA, groups), jnp.int32)
     row = iota((EXTRA, groups), 0)
     for k in range(ccap):
-        blank = jnp.where(row == 2 * k, places[k : k + 1, :] // 32, blank)
-        blank = jnp.where(row == 2 * k + 1, places[k : k + 1, :] % 32, blank)
-    code = jnp.concatenate([blank.astype(F32), jnp.zeros((EXTRA, width - groups), F32)], axis=1).astype(BF16)
-    out_ref[hot_each + cold_rows :, :] = code
-
-
-def last_kernel(groups, ccap, got_ref, hot_ref, cold_ref):
+        code = jnp.where(row == 2 * k, list_ref[k : k + 1, :] // 32, code)
+        code = jnp.where(row == 2 * k + 1, list_ref[k : k + 1, :] % 32, code)
+    code = jnp.concatenate([code.astype(F32), jnp.zeros((EXTRA, width - groups), F32)], axis=1)
+    cold_ref[cold_rows:, :] = code.astype(BF16)
+
+
+def cold_kernel(groups, ccap, got_ref, cold_ref):
     members, each, width = got_ref.shape
-    hot_each = hot_ref.shape[0] // members
     cold_local = cold_ref.shape[0]
     last_row = each - EXTRA
     total = jnp.zeros((cold_local, width), F32)
     for m in range(members):
-        hot_ref[m * hot_each : (m + 1) * hot_each, :] = got_ref[m, 0:hot_each, :].astype(F32)
         code = got_ref[m, last_row:, :].astype(F32)
         to = [code[2 * k : 2 * k + 1, :groups] * 32.0 + code[2 * k + 1 : 2 * k + 2, :groups] for k in range(ccap)]
         to = jnp.concatenate(to, axis=1).astype(jnp.int32)
-        total += dot(short_hits(iota((cold_local, to.shape[1]), 0), to), got_ref[m, hot_each:last_row, :])
+        total += dot(short_hits(iota((cold_local, to.shape[1]), 0), to), got_ref[m, 0:last_row, :])
     cold_ref[...] = total
+
+
+def share_kernel(start, got_ref, out_ref):
+    members, rows, _ = out_ref.shape
+    for m in range(members):
+        out_ref[m] = got_ref[start : start + rows, :]
+
+
+def widen_kernel(got_ref, out_ref):
+    out_ref[...] = got_ref[0 : out_ref.shape[0], :].astype(F32)
 
 
 def per_device(
@@ -373,28 +372,28 @@
     )
     summands = exchange_rows(to_groups, 2)
     my_chunk, my_cold = call(
-        functools.partial(finish_kernel, chunk, slot, ccap),
+        functools.partial(finish_kernel, chunk, slot),
         "finish",
-        (shape(groups * chunk, width), shape(cold_slots, width)),
-        (summands,),
+        (shape(groups * chunk, width), shape(cold_slots + EXTRA, width)),
+        (summands, cold_list),
         2 * groups * slot * width * cold_slots,
     )
     chunks = exchange_rows(my_chunk, 4)
-    warm_grad, to_all = call(
-        spread_kernel,
-        "spread",
-        (shape(warm_local, width, kind=F32), shape(hot_each + cold_slots + EXTRA, width)),
-        (chunks, my_cold, cold_list),
-        2 * groups * slot * width,
-    )
-    last = lax.all_gather(to_all, "member", axis=0)
-    hot_grad, cold_grad = call(
-        functools.partial(last_kernel, groups, ccap),
-        "last",
-        (shape(hot_rows, width, kind=F32), shape(cold_local, width, kind=F32)),
-        (last,),
+    all_cold = lax.all_gather(my_cold, "member", axis=0)
+    chunks, all_cold = lax.optimization_barrier((chunks, all_cold))
+    cold_grad = call(
+        functools.partial(cold_kernel, groups, ccap),
+        "cold",
+        shape(cold_local, width, kind=F32),
+        (all_cold,),
         2 * cold_local * members * cold_slots * width,
     )
+    my_hot = call(
+        functools.partial(share_kernel, warm_local), "share", shape(members, hot_each, width), (chunks,), hot_rows * width
+    )
+    all_hot = exchange(my_hot, "member")
+    warm_grad = call(widen_kernel, "warm", shape(warm_local, width, kind=F32), (chunks,), warm_local * width)
+    hot_grad = call(widen_kernel, "hot", shape(hot_rows, width, kind=F32), (all_hot.reshape(hot_rows, width),), hot_rows * width)
     return hot_grad, warm_grad, cold_grad
 
 

time: 150 us -> 146 us (0.973)
  blocking collectives: 82 us -> 55 us
  starting transfers between devices: 27.7 us -> 42.3 us
  waiting for transfers between devices: 7.85 us -> 14.2 us
  Pallas kernels: 24.4 us -> 26.4 us
    all_to_all x3 -> x2, blocking collectives: 65.1 us -> 40.1 us  [exchange(): return lax.all_to_all(x, axis, split_axis=0, concat_axis=0, tiled=True)]
    all_to_all x2 -> x4, starting transfers between devices: 27.7 us -> 42.3 us  [exchange(): return lax.all_to_all(x, axis, split_axis=0, concat_axis=0, tiled=True)]
    all_to_all x2 -> x4, waiting for transfers between devices: 7.85 us -> 14.2 us  [exchange(): return lax.all_to_all(x, axis, split_axis=0, concat_axis=0, tiled=True)]
    pallas_call x8 -> x10, Pallas kernels: 24.4 us -> 26.4 us  [call(): pl.pallas_call(kernel, name=name, out_shape=out_shape, in_specs=[VMEM] *...]
    all_gather x1, blocking collectives: 16.9 us -> 14.9 us  [per_device(): all_cold = lax.all_gather(my_cold, 'member', axis=0)]
  transfers between devices with their start and end apart: 2 -> 4, of which waited for: 2 -> 4; matrix products, arithmetic and copies ran while one was open for 1% -> 1% of each run, Pallas kernels for 4% -> 6%
where the time goes in v4:
time: 146 us; the launch traced here: 145 us
  blocking collectives  55 us (38%)
  starting transfers between devices  42.3 us (29%)
  Pallas kernels  26.4 us (18%)
  waiting for transfers between devices  14.2 us (10%)
  local copies, waits for them, and re-layouts  6.36 us (4%)
    all_to_all x4, starting transfers between devices, exchange(): return lax.all_to_all(x, axis, split_axis=0, concat_axis=0, tiled=True)  42.3 us
    all_to_all x2, blocking collectives, exchange(): return lax.all_to_all(x, axis, split_axis=0, concat_axis=0, tiled=True)  40.1 us
    pallas_call x10, Pallas kernels, call(): pl.pallas_call(kernel, name=name, out_shape=out_shape, in_specs=[VMEM] *...  26.4 us
    all_gather x1, blocking collectives, per_device(): all_cold = lax.all_gather(my_cold, 'member', axis=0)  14.9 us
    all_to_all x4, waiting for transfers between devices, exchange(): return lax.all_to_all(x, axis, split_axis=0, concat_axis=0, tiled=True)  14.2 us
    unnamed x22, local copies, waits for them, and re-layouts  4.96 us
  transfers between devices with their start and end apart: 4, of which 4 were waited for; matrix products, arithmetic and copies ran while one was open for 1% of the time, Pallas kernels for 6%

profile of v4, /device:TPU:1, one launch (start us, length us, event | category | flops | bytes accessed | tf_op | source)
XLA Modules:
  0.0 145.1 jit_solution(16379690124524562750)
XLA Ops:
  0.6 0.0 copy-start.3
  0.6 0.9 copy-done.3
  1.6 0.0 copy-start.8
  1.6 0.7 copy-done.8
  2.3 1.2 serve_warm.1
  3.4 13.8 %all-to-all-start = ((bf16[8,64,128]{2,1,0:T(8,128)(2,1)}), bf16[8,64,128]{2,1,0:T(8,128)(2,1)S(1)}, u32[]{:S(2)}, u32[]{:S(2)}) async-start(bf16[8,64,128]{2,1,0:T(8,128)(2,1)} %serve_warm.1), calls=%async_computation | async-start | bytes 262144 | tf_op jit(solution)/shard_map/all_to_all | solution.py:339
  17.2 0.7 reshape.51.w_out_ref
  17.9 0.7 reshape.49.bias_ref
  18.6 0.0 copy-start
  18.6 0.9 copy-done
  19.6 0.0 copy-start.1
  19.6 0.7 copy-done.1
  20.2 1.0 serve_cold.1
  21.2 1.3 all-to-all-done
  22.5 13.9 %all-to-all-start.1 = ((bf16[96,2,128]{2,1,0:T(2,128)(2,1)}), bf16[96,2,128]{2,1,0:T(2,128)(2,1)S(1)}, u32[]{:S(2)}, u32[]{:S(2)}) async-start(bf16[96,2,128]{2,1,0:T(2,128)(2,1)} %bitcast.5), calls=%async_computation.1 | async-start | bytes 98304 | tf_op jit(solution)/shard_map/all_to_all | solution.py:339
  36.4 0.0 copy-start.4
  36.4 0.9 copy-done.4
  37.4 0.0 copy-start.5
  37.4 0.7 copy-done.5
  38.1 0.0 copy-start.6
  38.1 0.0 copy-start.7
  38.1 0.0 copy-start.10
  38.1 4.5 %lookup.1.found_ref = bf16[256,2560]{1,0:T(8,128)(2,1)S(1)} custom-call(bf16[1024,128]{1,0:T(8,128)(2,1)S(1)} %copy-done.4, bf16[512,128]{1,0:T(8,128)(2,1)S(1)} %bitcast.24, s32[20,256]{1,0:T(8,128)S(1)} %bitcast.28), custom_call_target="tpu_custom_call" | custom-call | flops 4026531840 | bytes 2000000 | tf_op jit(solution)/shard_map/lookup/pallas_call | solution.py:178
  42.6 6.5 %all-to-all-done.1 = bf16[96,2,128]{2,1,0:T(2,128)(2,1)S(1)} async-done(((bf16[96,2,128]{2,1,0:T(2,128)(2,1)}), bf16[96,2,128]{2,1,0:T(2,128)(2,1)S(1)}, u32[]{:S(2)}, u32[]{:S(2)}) %all-to-all-start.1) | async-done | bytes 49184 | tf_op jit(solution)/shard_map/all_to_all | solution.py:339
  49.1 0.0 copy-done.6
  49.1 0.0 copy-done.7
  49.1 0.0 copy-done.10
  49.1 0.0 copy-start.9
  49.2 12.2 %tower.1 = (bf16[8,192,128]{2,1,0:T(8,128)(2,1)S(1)}, bf16[192,128]{1,0:T(8,128)(2,1)S(1)}) custom-call(bf16[256,2560]{1,0:T(8,128)(2,1)S(1)} %lookup.1.found_ref, bf16[192,128]{1,0:T(8,128)(2,1)S(1)} %bitcast.25, s32[20,256]{1,0:T(8,128)S(1)} %bitcast.29, s32[1,256]{1,0:T(1,128)S(1)} %bitcast.33, f32[1,2560]{1,0:T(1,128)S(1)} %reshape.49.bias_ref, ...), custom_call_target="tpu_custom_call" | custom-call | flops 13086228480 | bytes 2000000 | tf_op jit(solution)/shard_map/tower/pallas_call | solution.py:178
  61.4 12.8 %all_to_all.30 = bf16[8,192,128]{2,1,0:T(8,128)(2,1)S(1)} all-to-all(bf16[8,192,128]{2,1,0:T(8,128)(2,1)S(1)} %get-tuple-element.9), channel_id=1, replica_groups=mesh['group'=96,'member'=8] {'member'}, dimensions={0} | all-to-all | bytes 786432 | tf_op jit(solution)/shard_map/all_to_all | solution.py:339
  74.2 0.0 copy-done.9
  74.2 0.0 copy-start.2
  74.3 1.9 %owner.1 = bf16[1344,128]{1,0:T(8,128)(2,1)S(1)} custom-call(bf16[1536,128]{1,0:T(8,128)(2,1)S(1)} %bitcast.22, bf16[192,128]{1,0:T(8,128)(2,1)S(1)} %get-tuple-element.10.cold_ref, s32[8,64]{1,0:T(8,128)S(1)} %bitcast.32), custom_call_target="tpu_custom_call" | custom-call | flops 594542592 | bytes 2000000 | tf_op jit(solution)/shard_map/owner/pallas_call | solution.py:178
  76.1 27.2 %all_to_all.31 = bf16[672,2,128]{2,1,0:T(2,128)(2,1)S(1)} all-to-all(bf16[672,2,128]{2,1,0:T(2,128)(2,1)S(1)} %bitcast.23), channel_id=1, replica_groups=mesh['group'=96,'member'=8] {'group'}, dimensions={0} | all-to-all | bytes 688128 | tf_op jit(solution)/shard_map/all_to_all | solution.py:339
  103.3 0.0 copy-done.2
  103.3 1.2 finish.1
  104.6 7.3 %all-to-all-start.4 = ((bf16[288,4,128]{2,1,0:T(4,128)(2,1)}), bf16[288,4,128]{2,1,0:T(4,128)(2,1)S(1)}, u32[]{:S(2)}, u32[]{:S(2)}) async-start(bf16[288,4,128]{2,1,0:T(4,128)(2,1)} %bitcast.12), calls=%async_computation.4 | async-start | bytes 589824 | tf_op jit(solution)/shard_map/all_to_all | solution.py:339
  111.9 14.9 %all-gather = bf16[1664,128]{1,0:T(8,128)(2,1)S(1)} all-gather(bf16[208,128]{1,0:T(8,128)(2,1)S(1)} %get-tuple-element.12), channel_id=2, replica_groups=mesh['group'=96,'member'=8] {'member'}, dimensions={0}, use_global_device_ids=true | all-gather | bytes 479232 | tf_op jit(solution)/shard_map/all_gather | solution.py:382
  126.8 2.8 %all-to-all-done.4 = bf16[288,4,128]{2,1,0:T(4,128)(2,1)S(1)} async-done(((bf16[288,4,128]{2,1,0:T(4,128)(2,1)}), bf16[288,4,128]{2,1,0:T(4,128)(2,1)S(1)}, u32[]{:S(2)}, u32[]{:S(2)}) %all-to-all-start.4) | async-done | bytes 294944 | tf_op jit(solution)/shard_map/all_to_all | solution.py:339
  129.6 0.7 share.1
  130.4 7.3 %all-to-all-start.5 = ((bf16[8,128,128]{2,1,0:T(8,128)(2,1)}), bf16[8,128,128]{2,1,0:T(8,128)(2,1)S(1)}, u32[]{:S(2)}, u32[]{:S(2)}) async-start(bf16[8,128,128]{2,1,0:T(8,128)(2,1)} %share.1), calls=%async_computation.5 | async-start | bytes 524288 | tf_op jit(solution)/shard_map/all_to_all | solution.py:339
  137.7 0.8 warm.1
  138.5 2.1 %cold.1 = f32[1024,128]{1,0:T(8,128)} custom-call(bf16[8,208,128]{2,1,0:T(8,128)(2,1)S(1)} %bitcast.21), custom_call_target="tpu_custom_call" | custom-call | flops 402653184 | bytes 2000000 | tf_op jit(solution)/shard_map/cold/pallas_call | solution.py:178
  140.6 3.6 %all-to-all-done.5 = bf16[8,128,128]{2,1,0:T(8,128)(2,1)S(1)} async-done(((bf16[8,128,128]{2,1,0:T(8,128)(2,1)}), bf16[8,128,128]{2,1,0:T(8,128)(2,1)S(1)}, u32[]{:S(2)}, u32[]{:S(2)}) %all-to-all-start.5) | async-done | bytes 262176 | tf_op jit(solution)/shard_map/all_to_all | solution.py:339
  144.2 0.8 hot.1
Async XLA Ops:
  0.6 1.0 copy-start.3
  1.6 0.7 copy-start.8
  3.4 19.1 %all-to-all-start = ((bf16[8,64,128]{2,1,0:T(8,128)(2,1)}), bf16[8,64,128]{2,1,0:T(8,128)(2,1)S(1)}, u32[]{:S(2)}, u32[]{:S(2)}) async-start(bf16[8,64,128]{2,1,0:T(8,128)(2,1)} %serve_warm.1), calls=%async_computation | async-start | bytes 262144 | tf_op jit(solution)/shard_map/all_to_all | solution.py:339
  18.6 0.9 copy-start
  19.6 0.7 copy-start.1
  22.5 26.6 %all-to-all-start.1 = ((bf16[96,2,128]{2,1,0:T(2,128)(2,1)}), bf16[96,2,128]{2,1,0:T(2,128)(2,1)S(1)}, u32[]{:S(2)}, u32[]{:S(2)}) async-start(bf16[96,2,128]{2,1,0:T(2,128)(2,1)} %bitcast.5), calls=%async_computation.1 | async-start | bytes 98304 | tf_op jit(solution)/shard_map/all_to_all | solution.py:339
  36.4 1.0 copy-start.4
  37.4 0.7 copy-start.5
  38.1 11.0 %copy-start.6 = (s32[256,20]{0,1:T(8,128)S(1)}, s32[256,20]{0,1:T(8,128)}, u32[]{:S(2)}) copy-start(s32[256,20]{0,1:T(8,128)} %param.18) | copy-start | bytes 61444
  38.1 11.0 %copy-start.7 = (f32[1024]{0:T(1024)S(1)}, f32[1024]{0:T(1024)}, u32[]{:S(2)}) copy-start(f32[1024]{0:T(1024)} %param.24) | copy-start | bytes 12292
  38.1 11.0 %copy-start.10 = (s32[256]{0:T(256)S(1)}, s32[256]{0:T(256)}, u32[]{:S(2)}) copy-start(s32[256]{0:T(256)} %param.19) | copy-start | bytes 3076
  49.1 25.1 %copy-start.9 = (s32[1,1,8,64]{3,2,1,0:T(8,128)S(1)}, s32[1,1,8,64]{3,2,1,0:T(8,128)}, u32[]{:S(2)}) copy-start(s32[1,1,8,64]{3,2,1,0:T(8,128)} %param.16) | copy-start | bytes 6148
  74.2 29.1 %copy-start.2 = (s32[1,1,96,2]{2,3,1,0:T(2,128)S(1)}, s32[1,1,96,2]{2,3,1,0:T(2,128)}, u32[]{:S(2)}) copy-start(s32[1,1,96,2]{2,3,1,0:T(2,128)} %param.17) | copy-start | bytes 2308
  104.6 25.0 %all-to-all-start.4 = ((bf16[288,4,128]{2,1,0:T(4,128)(2,1)}), bf16[288,4,128]{2,1,0:T(4,128)(2,1)S(1)}, u32[]{:S(2)}, u32[]{:S(2)}) async-start(bf16[288,4,128]{2,1,0:T(4,128)(2,1)} %bitcast.12), calls=%async_computation.4 | async-start | bytes 589824 | tf_op jit(solution)/shard_map/all_to_all | solution.py:339
  130.4 13.9 %all-to-all-start.5 = ((bf16[8,128,128]{2,1,0:T(8,128)(2,1)}), bf16[8,128,128]{2,1,0:T(8,128)(2,1)S(1)}, u32[]{:S(2)}, u32[]{:S(2)}) async-start(bf16[8,128,128]{2,1,0:T(8,128)(2,1)} %share.1), calls=%async_computation.5 | async-start | bytes 524288 | tf_op jit(solution)/shard_map/all_to_all | solution.py:339

commit v5 on v4

--- a/solution.py
+++ b/solution.py
@@ -11,7 +11,7 @@
 BF16 = jnp.bfloat16
 VMEM = pl.BlockSpec(memory_space=pltpu.VMEM)
 HBM = pl.BlockSpec(memory_space=pltpu.HBM)
-TILE = 512
+TILE = 1280
 LANES = 128
 EXTRA = 16
 
@@ -234,7 +234,7 @@
     )
 
 
-def serve_cold_kernel(table_ref, list_ref, out_ref):
+def serve_cold_kernel(table_ref, list_ref, out_ref, code_ref):
     ccap, groups = list_ref.shape
     shape = (out_ref.shape[0], groups)
     row, group = iota(shape, 0), iota(shape, 1)
@@ -243,13 +243,26 @@
         ids = jnp.where((row // ccap == group) & (row % ccap == k), list_ref[k : k + 1, :], ids)
     ids = jnp.sum(ids, axis=1, keepdims=True)
     out_ref[...] = dot(short_hits(iota((shape[0], table_ref.shape[0]), 1), ids), table_ref[...]).astype(BF16)
-
-
-def serve_warm_kernel(table_ref, list_ref, out_ref):
+    code = jnp.zeros((EXTRA, groups), jnp.int32)
+    row = iota((EXTRA, groups), 0)
+    for k in range(ccap):
+        code = jnp.where(row == 2 * k, list_ref[k : k + 1, :] // 32, code)
+        code = jnp.where(row == 2 * k + 1, list_ref[k : k + 1, :] % 32, code)
+    code = jnp.concatenate([code.astype(F32), jnp.zeros((EXTRA, code_ref.shape[1] - groups), F32)], axis=1)
+    code_ref[...] = code.astype(BF16)
+
+
+def serve_warm_kernel(list_hbm, table_hbm, out_ref, list_ref, table_ref, sems):
+    list_copy = pltpu.make_async_copy(list_hbm, list_ref, sems.at[0])
+    table_copy = pltpu.make_async_copy(table_hbm, table_ref, sems.at[1])
+    list_copy.start()
+    table_copy.start()
+    list_copy.wait()
     members, wcap = list_ref.shape
+    found = [short_hits(iota((wcap, table_ref.shape[0]), 1), column_of(list_ref[m : m + 1, :])) for m in range(members)]
+    table_copy.wait()
     for m in range(members):
-        ids = column_of(list_ref[m : m + 1, :])
-        out_ref[m] = dot(short_hits(iota((wcap, table_ref.shape[0]), 1), ids), table_ref[...]).astype(BF16)
+        out_ref[m] = dot(found[m], table_ref[...]).astype(BF16)
 
 
 def owner_kernel(warm_local, chunk, slot, groups, got_ref, cold_ref, list_ref, out_ref):
@@ -269,7 +282,7 @@
     out_ref[...] = out.astype(BF16)
 
 
-def finish_kernel(chunk, slot, got_ref, list_ref, chunk_ref, cold_ref):
+def finish_kernel(chunk, slot, ccap, got_ref, code_ref, chunk_ref, cold_ref):
     total_rows = got_ref.shape[0]
     groups = total_rows // slot
     rows = up(chunk, 16)
@@ -278,19 +291,12 @@
     summed = dot(hits(own, iota(shape, 1) % slot), got_ref[...]).astype(BF16)
     place = iota((groups * chunk, rows), 0) % chunk
     chunk_ref[...] = dot(hits(place, iota((groups * chunk, rows), 1)), summed).astype(BF16)
-    ccap = list_ref.shape[0]
-    cold_rows, width = groups * ccap, cold_ref.shape[1]
+    cold_rows = groups * ccap
     row = iota((cold_rows, 1), 0)
     wanted = row % groups * slot + chunk + row // groups
     picked = dot(hits(wanted, iota((cold_rows, total_rows), 1)), got_ref[...])
     cold_ref[0:cold_rows, :] = picked.astype(BF16)
-    code = jnp.zeros((EXTRA, groups), jnp.int32)
-    row = iota((EXTRA, groups), 0)
-    for k in range(ccap):
-        code = jnp.where(row == 2 * k, list_ref[k : k + 1, :] // 32, code)
-        code = jnp.where(row == 2 * k + 1, list_ref[k : k + 1, :] % 32, code)
-    code = jnp.concatenate([code.astype(F32), jnp.zeros((EXTRA, width - groups), F32)], axis=1)
-    cold_ref[cold_rows:, :] = code.astype(BF16)
+    cold_ref[cold_rows:, :] = code_ref[...]
 
 
 def cold_kernel(groups, ccap, got_ref, cold_ref):
@@ -345,14 +351,21 @@
     def shape(*dims, kind=BF16):
         return jax.ShapeDtypeStruct(dims, kind)
 
-    cold_wanted = call(
-        serve_cold_kernel, "serve_cold", shape(cold_slots, width), (cold_table, cold_list),
+    cold_wanted, code = call(
+        serve_cold_kernel, "serve_cold", (shape(cold_slots, width), shape(EXTRA, width)), (cold_table, cold_list),
         2 * cold_slots * cold_local * width,
     )
     cold_fetched = exchange_rows(cold_wanted, ccap)
     warm_wanted = call(
-        serve_warm_kernel, "serve_warm", shape(members, wcap, width), (warm_table, warm_list),
+        serve_warm_kernel, "serve_warm", shape(members, wcap, width), (warm_list, warm_table),
         2 * warm_slots * warm_local * width,
+        [
+            pltpu.VMEM((members, wcap), jnp.int32),
+            pltpu.VMEM((warm_local, width), BF16),
+            pltpu.SemaphoreType.DMA((2,)),
+        ],
+        60,
+        apart=2,
     )
     warm_fetched = exchange(warm_wanted, "member").reshape(warm_slots, width)
     found = lookup(hot_table, warm_fetched, ids)
@@ -372,10 +385,10 @@
     )
     summands = exchange_rows(to_groups, 2)
     my_chunk, my_cold = call(
-        functools.partial(finish_kernel, chunk, slot),
+        functools.partial(finish_kernel, chunk, slot, ccap),
         "finish",
         (shape(groups * chunk, width), shape(cold_slots + EXTRA, width)),
-        (summands, cold_list),
+        (summands, code),
         2 * groups * slot * width * cold_slots,
     )
     chunks = exchange_rows(my_chunk, 4)

time: 146 us -> 144 us (0.986)
  local copies, waits for them, and re-layouts: 6.36 us -> 4.72 us
    unnamed x22 -> x16, local copies, waits for them, and re-layouts: 4.96 us -> 3.32 us
where the time goes in v5:
time: 144 us; the launch traced here: 143 us
  blocking collectives  55 us (38%)
  starting transfers between devices  42.3 us (29%)
  Pallas kernels  26 us (18%)
  waiting for transfers between devices  14.2 us (10%)
  local copies, waits for them, and re-layouts  4.72 us (3%)
    all_to_all x4, starting transfers between devices, exchange(): return lax.all_to_all(x, axis, split_axis=0, concat_axis=0, tiled=True)  42.3 us
    all_to_all x2, blocking collectives, exchange(): return lax.all_to_all(x, axis, split_axis=0, concat_axis=0, tiled=True)  40.1 us
    pallas_call x10, Pallas kernels, call(): pl.pallas_call(kernel, name=name, out_shape=out_shape, in_specs=[VMEM] *...  26 us
    all_gather x1, blocking collectives, per_device(): all_cold = lax.all_gather(my_cold, 'member', axis=0)  14.9 us
    all_to_all x4, waiting for transfers between devices, exchange(): return lax.all_to_all(x, axis, split_axis=0, concat_axis=0, tiled=True)  14.2 us
    unnamed x16, local copies, waits for them, and re-layouts  3.32 us
  transfers between devices with their start and end apart: 4, of which 4 were waited for; matrix products, arithmetic and copies ran while one was open for 1% of the time, Pallas kernels for 6%

profile of v5, /device:TPU:1, one launch (start us, length us, event | category | flops | bytes accessed | tf_op | source)
XLA Modules:
  0.0 143.0 jit_solution(3996994884365260407)
XLA Ops:
  0.6 2.1 %serve_warm.1 = bf16[8,64,128]{2,1,0:T(8,128)(2,1)} custom-call(s32[8,64]{1,0:T(8,128)} %bitcast.30, bf16[1024,128]{1,0:T(8,128)(2,1)} %table_hbm.1), custom_call_target="tpu_custom_call" | custom-call | flops 134217728 | bytes 2000000 | tf_op jit(solution)/shard_map/serve_warm/pallas_call | solution.py:178
  2.7 13.8 %all-to-all-start = ((bf16[8,64,128]{2,1,0:T(8,128)(2,1)}), bf16[8,64,128]{2,1,0:T(8,128)(2,1)S(1)}, u32[]{:S(2)}, u32[]{:S(2)}) async-start(bf16[8,64,128]{2,1,0:T(8,128)(2,1)} %serve_warm.1), calls=%async_computation | async-start | bytes 262144 | tf_op jit(solution)/shard_map/all_to_all | solution.py:345
  16.5 0.7 reshape.51.w_out_ref
  17.2 0.7 reshape.49.bias_ref
  17.9 0.0 copy-start
  17.9 0.9 copy-done
  18.9 0.0 copy-start.1
  18.9 0.7 copy-done.1
  19.5 1.0 serve_cold.1
  20.5 1.3 all-to-all-done
  21.8 13.9 %all-to-all-start.1 = ((bf16[96,2,128]{2,1,0:T(2,128)(2,1)}), bf16[96,2,128]{2,1,0:T(2,128)(2,1)S(1)}, u32[]{:S(2)}, u32[]{:S(2)}) async-start(bf16[96,2,128]{2,1,0:T(2,128)(2,1)} %bitcast.5), calls=%async_computation.1 | async-start | bytes 98304 | tf_op jit(solution)/shard_map/all_to_all | solution.py:345
  35.7 0.0 copy-start.2
  35.7 0.9 copy-done.2
  36.7 0.0 copy-start.3
  36.7 0.7 copy-done.3
  37.4 0.0 copy-start.4
  37.4 0.0 copy-start.5
  37.4 0.0 copy-start.7
  37.4 4.5 %lookup.1.found_ref = bf16[256,2560]{1,0:T(8,128)(2,1)S(1)} custom-call(bf16[1024,128]{1,0:T(8,128)(2,1)S(1)} %copy-done.2, bf16[512,128]{1,0:T(8,128)(2,1)S(1)} %bitcast.24, s32[20,256]{1,0:T(8,128)S(1)} %bitcast.27), custom_call_target="tpu_custom_call" | custom-call | flops 4026531840 | bytes 2000000 | tf_op jit(solution)/shard_map/lookup/pallas_call | solution.py:178
  41.9 6.5 %all-to-all-done.1 = bf16[96,2,128]{2,1,0:T(2,128)(2,1)S(1)} async-done(((bf16[96,2,128]{2,1,0:T(2,128)(2,1)}), bf16[96,2,128]{2,1,0:T(2,128)(2,1)S(1)}, u32[]{:S(2)}, u32[]{:S(2)}) %all-to-all-start.1) | async-done | bytes 49184 | tf_op jit(solution)/shard_map/all_to_all | solution.py:345
  48.4 0.0 copy-done.4
  48.4 0.0 copy-done.5
  48.4 0.0 copy-done.7
  48.4 0.0 copy-start.6
  48.5 10.9 %tower.1 = (bf16[8,192,128]{2,1,0:T(8,128)(2,1)S(1)}, bf16[192,128]{1,0:T(8,128)(2,1)S(1)}) custom-call(bf16[256,2560]{1,0:T(8,128)(2,1)S(1)} %lookup.1.found_ref, bf16[192,128]{1,0:T(8,128)(2,1)S(1)} %bitcast.25, s32[20,256]{1,0:T(8,128)S(1)} %bitcast.28, s32[1,256]{1,0:T(1,128)S(1)} %bitcast.32, f32[1,2560]{1,0:T(1,128)S(1)} %reshape.49.bias_ref, ...), custom_call_target="tpu_custom_call" | custom-call | flops 13086228480 | bytes 2000000 | tf_op jit(solution)/shard_map/tower/pallas_call | solution.py:178
  59.4 12.8 %all_to_all.30 = bf16[8,192,128]{2,1,0:T(8,128)(2,1)S(1)} all-to-all(bf16[8,192,128]{2,1,0:T(8,128)(2,1)S(1)} %get-tuple-element.12), channel_id=1, replica_groups=mesh['group'=96,'member'=8] {'member'}, dimensions={0} | all-to-all | bytes 786432 | tf_op jit(solution)/shard_map/all_to_all | solution.py:345
  72.2 0.0 copy-done.6
  72.2 1.9 %owner.1 = bf16[1344,128]{1,0:T(8,128)(2,1)S(1)} custom-call(bf16[1536,128]{1,0:T(8,128)(2,1)S(1)} %bitcast.22, bf16[192,128]{1,0:T(8,128)(2,1)S(1)} %get-tuple-element.13.cold_ref, s32[8,64]{1,0:T(8,128)S(1)} %bitcast.31), custom_call_target="tpu_custom_call" | custom-call | flops 594542592 | bytes 2000000 | tf_op jit(solution)/shard_map/owner/pallas_call | solution.py:178
  74.1 27.2 %all_to_all.31 = bf16[672,2,128]{2,1,0:T(2,128)(2,1)S(1)} all-to-all(bf16[672,2,128]{2,1,0:T(2,128)(2,1)S(1)} %bitcast.23), channel_id=1, replica_groups=mesh['group'=96,'member'=8] {'group'}, dimensions={0} | all-to-all | bytes 688128 | tf_op jit(solution)/shard_map/all_to_all | solution.py:345
  101.3 1.2 finish.1
  102.6 7.3 %all-to-all-start.4 = ((bf16[288,4,128]{2,1,0:T(4,128)(2,1)}), bf16[288,4,128]{2,1,0:T(4,128)(2,1)S(1)}, u32[]{:S(2)}, u32[]{:S(2)}) async-start(bf16[288,4,128]{2,1,0:T(4,128)(2,1)} %bitcast.12), calls=%async_computation.4 | async-start | bytes 589824 | tf_op jit(solution)/shard_map/all_to_all | solution.py:345
  109.9 14.9 %all-gather = bf16[1664,128]{1,0:T(8,128)(2,1)S(1)} all-gather(bf16[208,128]{1,0:T(8,128)(2,1)S(1)} %get-tuple-element.16), channel_id=2, replica_groups=mesh['group'=96,'member'=8] {'member'}, dimensions={0}, use_global_device_ids=true | all-gather | bytes 479232 | tf_op jit(solution)/shard_map/all_gather | solution.py:395
  124.8 2.8 %all-to-all-done.4 = bf16[288,4,128]{2,1,0:T(4,128)(2,1)S(1)} async-done(((bf16[288,4,128]{2,1,0:T(4,128)(2,1)}), bf16[288,4,128]{2,1,0:T(4,128)(2,1)S(1)}, u32[]{:S(2)}, u32[]{:S(2)}) %all-to-all-start.4) | async-done | bytes 294944 | tf_op jit(solution)/shard_map/all_to_all | solution.py:345
  127.6 0.7 share.1
  128.3 7.3 %all-to-all-start.5 = ((bf16[8,128,128]{2,1,0:T(8,128)(2,1)}), bf16[8,128,128]{2,1,0:T(8,128)(2,1)S(1)}, u32[]{:S(2)}, u32[]{:S(2)}) async-start(bf16[8,128,128]{2,1,0:T(8,128)(2,1)} %share.1), calls=%async_computation.5 | async-start | bytes 524288 | tf_op jit(solution)/shard_map/all_to_all | solution.py:345
  135.7 0.8 warm.1
  136.5 2.1 %cold.1 = f32[1024,128]{1,0:T(8,128)} custom-call(bf16[8,208,128]{2,1,0:T(8,128)(2,1)S(1)} %bitcast.21), custom_call_target="tpu_custom_call" | custom-call | flops 402653184 | bytes 2000000 | tf_op jit(solution)/shard_map/cold/pallas_call | solution.py:178
  138.6 3.6 %all-to-all-done.5 = bf16[8,128,128]{2,1,0:T(8,128)(2,1)S(1)} async-done(((bf16[8,128,128]{2,1,0:T(8,128)(2,1)}), bf16[8,128,128]{2,1,0:T(8,128)(2,1)S(1)}, u32[]{:S(2)}, u32[]{:S(2)}) %all-to-all-start.5) | async-done | bytes 262176 | tf_op jit(solution)/shard_map/all_to_all | solution.py:345
  142.2 0.8 hot.1
Async XLA Ops:
  2.7 19.1 %all-to-all-start = ((bf16[8,64,128]{2,1,0:T(8,128)(2,1)}), bf16[8,64,128]{2,1,0:T(8,128)(2,1)S(1)}, u32[]{:S(2)}, u32[]{:S(2)}) async-start(bf16[8,64,128]{2,1,0:T(8,128)(2,1)} %serve_warm.1), calls=%async_computation | async-start | bytes 262144 | tf_op jit(solution)/shard_map/all_to_all | solution.py:345
  17.9 0.9 copy-start
  18.9 0.7 copy-start.1
  21.8 26.6 %all-to-all-start.1 = ((bf16[96,2,128]{2,1,0:T(2,128)(2,1)}), bf16[96,2,128]{2,1,0:T(2,128)(2,1)S(1)}, u32[]{:S(2)}, u32[]{:S(2)}) async-start(bf16[96,2,128]{2,1,0:T(2,128)(2,1)} %bitcast.5), calls=%async_computation.1 | async-start | bytes 98304 | tf_op jit(solution)/shard_map/all_to_all | solution.py:345
  35.7 1.0 copy-start.2
  36.7 0.7 copy-start.3
  37.4 11.0 %copy-start.4 = (s32[256,20]{0,1:T(8,128)S(1)}, s32[256,20]{0,1:T(8,128)}, u32[]{:S(2)}) copy-start(s32[256,20]{0,1:T(8,128)} %param.18) | copy-start | bytes 61444
  37.4 11.0 %copy-start.5 = (f32[1024]{0:T(1024)S(1)}, f32[1024]{0:T(1024)}, u32[]{:S(2)}) copy-start(f32[1024]{0:T(1024)} %param.24) | copy-start | bytes 12292
  37.4 11.0 %copy-start.7 = (s32[256]{0:T(256)S(1)}, s32[256]{0:T(256)}, u32[]{:S(2)}) copy-start(s32[256]{0:T(256)} %param.19) | copy-start | bytes 3076
  48.4 23.8 %copy-start.6 = (s32[1,1,8,64]{3,2,1,0:T(8,128)S(1)}, s32[1,1,8,64]{3,2,1,0:T(8,128)}, u32[]{:S(2)}) copy-start(s32[1,1,8,64]{3,2,1,0:T(8,128)} %param.16) | copy-start | bytes 6148
  102.6 25.0 %all-to-all-start.4 = ((bf16[288,4,128]{2,1,0:T(4,128)(2,1)}), bf16[288,4,128]{2,1,0:T(4,128)(2,1)S(1)}, u32[]{:S(2)}, u32[]{:S(2)}) async-start(bf16[288,4,128]{2,1,0:T(4,128)(2,1)} %bitcast.12), calls=%async_computation.4 | async-start | bytes 589824 | tf_op jit(solution)/shard_map/all_to_all | solution.py:345
  128.3 13.9 %all-to-all-start.5 = ((bf16[8,128,128]{2,1,0:T(8,128)(2,1)}), bf16[8,128,128]{2,1,0:T(8,128)(2,1)S(1)}, u32[]{:S(2)}, u32[]{:S(2)}) async-start(bf16[8,128,128]{2,1,0:T(8,128)(2,1)} %share.1), calls=%async_computation.5 | async-start | bytes 524288 | tf_op jit(solution)/shard_map/all_to_all | solution.py:345
